TPU v7x, 32 devices: a whole 2x2x4 slice. The times are simulated.
32 devices in a mesh: visit: 8 (over z, x), patch: 4 (over y, core).
Axes of the slice: x: 2, y: 2, z: 4, core: 2. Of those that a mesh axis runs over, the one named last changes fastest.
Arguments:
- templates: float32 [8, 2, 64, 1024], P('visit', None, 'patch'), may hold values from -16 to 16, as said below
- owners: int32 [2], replicated, may hold values from 0 to 7, as said below
- science: float32 [2, 8, 64, 1024], P(None, 'visit', 'patch'), may hold values from -40 to 40
- sci_var: float32 [2, 8, 64, 1024], P(None, 'visit', 'patch'), may hold values from 0.03 to 0.3
- bad_pixels: int32 [2, 8, 64, 1024], P(None, 'visit', 'patch'), may hold values 0 or 1
Outputs:
- significance: float32 [2, 8, 64, 1024], P(None, 'visit', 'patch')
Inputs may be any that keep to these rules, and one draw needn't show every extreme that they name: `owners`: the steps' entries are distinct indices of stored tiles, one of them always 8 - 1. `templates`: variances (index 1) lie in 0.01 to 0.1.
All inputs are finite; a program needn't handle non-finite values. No bound on the sum of `bad_pixels` on one device may be relied on, other than what follows from the above.
Results may differ from a plain program's by a relative error of at most 0.0003.
Values sent between devices are 32-bit elements; how exact they have to be, the bound alone decides.
No kernel may reach another device: no remote copies, remote signals or barrier semaphores. Data moves between devices by JAX's collectives and lax.ppermute only.
A program may use at most 64 MiB of HBM per device.

v0:
```python
import jax
import jax.numpy as jnp
import numpy as np
from jax import lax
from jax.sharding import PartitionSpec as P

NPROF = 5
RAD = 10
STEPS = 2


ridge = 1.0


def from_root(block, axis, holder):
    block = jnp.where(lax.axis_index(axis) == holder, block, jnp.zeros_like(block))
    return lax.psum(block, axis)


def padded(cells, sides, width):
    for axis, dim in sides:
        count = lax.axis_size(axis)
        ends = count - 1
        head = lax.slice_in_dim(cells, 0, width, axis=dim)
        tail = lax.slice_in_dim(cells, cells.shape[dim] - width, cells.shape[dim], axis=dim)
        cells = jnp.concatenate(
            [
                lax.ppermute(tail, axis, [(i, (i + 1) % count) for i in range(ends)]),
                cells,
                lax.ppermute(head, axis, [((i + 1) % count, i) for i in range(ends)]),
            ],
            axis=dim,
        )
    return cells


def profile_table():
    offsets = np.arange(-RAD, RAD + 1) * 1.0
    recipe = [(1.0, 0), (1.5, 1), (2.0, 2), (3.0, 0), (4.0, 1)]
    profiles = []
    for spread, degree in recipe[:NPROF]:
        profile = offsets**degree * np.exp(-offsets * offsets / (2.0 * spread * spread))
        for earlier in profiles:
            profile = profile - np.dot(earlier, profile) * earlier
        profile = profile / np.sqrt(np.dot(profile, profile))
        profiles.append(profile)
    return np.stack(profiles)


def band_table(profiles, outputs, inputs):
    distance = jnp.arange(inputs)[None, :] - jnp.arange(outputs)[:, None]
    table = jnp.zeros((NPROF, outputs, inputs), jnp.float32)
    for offset in range(2 * RAD + 1):
        table = (
            table + profiles[:, offset, None, None] * (distance == offset).astype(jnp.float32)[None]
        )
    return table


def basis_images(extended):
    profiles = jnp.asarray(profile_table(), jnp.float32)
    height = extended.shape[0] - 2 * RAD
    across = extended.shape[1]
    block_width = 128
    block_count = across // block_width
    widened = jnp.pad(extended, ((0, 0), (RAD, RAD)))
    blocks = jnp.stack(
        [
            widened[:, start * block_width : start * block_width + block_width + 2 * RAD]
            for start in range(block_count)
        ]
    )
    col_table = jnp.transpose(band_table(profiles, block_width, block_width + 2 * RAD), (0, 2, 1))
    columns = jnp.einsum("srx,kxc->krsc", blocks, col_table, precision=lax.Precision.HIGHEST)
    columns = columns.reshape(NPROF, extended.shape[0], across)
    row_table = band_table(profiles, height, height + 2 * RAD)
    images = jnp.einsum("lhr,krc->klhc", row_table, columns, precision=lax.Precision.HIGHEST)
    return images.reshape(NPROF * NPROF, height, across)


def solve_kernel(normal_mat, normal_rhs):
    count = normal_mat.shape[0]
    factor = jnp.linalg.cholesky(normal_mat + ridge * jnp.eye(count, dtype=jnp.float32))
    return jax.scipy.linalg.cho_solve((factor, True), normal_rhs)


def finish_step(normal_mat, normal_rhs, flattened, usable, noise_var, image_sci):
    kernel_coef = jax.vmap(solve_kernel)(normal_mat, normal_rhs)
    fitted = jnp.einsum(
        "vb,bp->vp", kernel_coef, flattened, precision=lax.Precision.HIGHEST
    ).reshape(image_sci.shape)
    return usable * (image_sci - fitted) / jnp.sqrt(noise_var)


def shards(templates, owners, science, sci_var, bad_pixels):
    own_pair = templates[0]
    visit_count = science.shape[1]
    basis_count = NPROF * NPROF
    results = []
    for current in range(STEPS):
        owner_index = owners[current]
        arrived = from_root(own_pair, "visit", owner_index)
        extended = padded(arrived[0], (("patch", 0),), RAD)
        tile_var = arrived[1]
        images = basis_images(extended)
        flattened = images.reshape(basis_count, -1)
        usable = (1 - bad_pixels[current]).astype(jnp.float32)
        noise_var = sci_var[current] + tile_var[None]
        weight = usable / noise_var
        weighted = (images[None] * weight[:, None]).reshape(visit_count, basis_count, -1)
        normal_mat = jnp.einsum("vbp,cp->vbc", weighted, flattened, precision=lax.Precision.HIGHEST)
        normal_rhs = jnp.einsum(
            "cp,vp->vc",
            flattened,
            (weight * science[current]).reshape(visit_count, -1),
            precision=lax.Precision.HIGHEST,
        )
        summed_mat, summed_rhs = lax.psum((normal_mat, normal_rhs), "patch")
        results.append(
            finish_step(summed_mat, summed_rhs, flattened, usable, noise_var, science[current])
        )
    return jnp.stack(results)


def solution(mesh):
    return jax.shard_map(
        shards,
        mesh=mesh,
        in_specs=(
            P("visit", None, "patch", None),
            P(),
            P(None, "visit", "patch", None),
            P(None, "visit", "patch", None),
            P(None, "visit", "patch", None),
        ),
        out_specs=P(None, "visit", "patch", None),
        check_vma=False,
    )
```

profile of v0, /device:TPU:0, one launch (start us, length us, event | category | flops | bytes accessed | tf_op | source)
XLA Modules:
  0.0 171.9 jit_solution(14220269415641050189)
XLA Ops:
  6.8 1.4 fusion.136
  9.5 1.6 select_bitcast_fusion.1
  11.8 0.2 multiply_add_fusion.1
  12.0 0.7 multiply_add_fusion
  12.7 72.1 %all-reduce.6.cloned.1.call-done = (f32[2,16,1024]{2,1,0:T(8,128)}, f32[2,16,1024]{2,1,0:T(8,128)}) async-done(((f32[2,16,1024]{2,1,0:T(8,128)}, f32[2,16,1024]{2,1,0:T(8,128)}), (f32[2,16,1024]{2,1,0:T(8,128)}, f32[2,16,1024]{2,1,0:T(8,128)})) %all-reduce.6.cloned.1.call-update) | async-done | bytes 262160 | tf_op jit(solution)/shard_map/psum | solution.py:17
  84.8 0.9 slice_bitcast_fusion.4
  85.7 1.3 collective-permute-start.2
  87.0 1.3 collective-permute-start.3
  88.3 0.9 slice_bitcast_fusion.7
  89.3 4.7 %collective-permute-start = (f32[10,1024]{1,0:T(8,128)S(1)}, f32[10,1024]{1,0:T(8,128)S(1)}, u32[]{:S(2)}, u32[]{:S(2)}) collective-permute-start(f32[10,1024]{1,0:T(8,128)S(1)} %get-tuple-element.21), channel_id=1, source_target_pairs={{0,1},{1,2},{2,3},{4,5},{5,6},{6,7},{8,9},{9,10},{10,11},{12,13},{... | collective-permute-start | bytes 122888 | tf_op jit(solution)/shard_map/ppermute | solution.py:28
  94.0 1.3 collective-permute-start.1
  95.3 1.0 fusion.59
  96.3 0.7 copy.29
  97.0 0.7 copy.33
  97.7 0.7 collective-permute-done.1
  98.7 0.1 fusion.77
  98.7 0.1 fusion.76
  98.8 0.1 fusion.75
  99.0 0.1 fusion.63
  99.6 0.1 fusion.67
  99.7 1.0 convolution_bitcast_fusion
  100.7 0.1 copy.15
  100.8 0.1 reshape.751
  101.0 1.0 convolution_bitcast_fusion.1
  101.9 0.1 copy.12
  102.1 0.1 reshape.740
  102.2 1.6 bitcast_multiply_fusion.1
  103.8 0.1 slice_bitcast_fusion.1
  103.9 0.2 pad.18
  104.1 1.6 bitcast_multiply_fusion
  105.8 0.1 slice_bitcast_fusion
  105.9 0.2 pad.20
  106.1 0.3 pad.17
  106.4 1.2 copy.27
  107.6 1.2 copy.28
  108.9 1.8 %convolution_bitcast_fusion.3 = f32[1,25,25]{1,2,0:T(8,128)S(1)} fusion(f32[25,16384]{1,0:T(8,128)S(1)} %bitcast.318, f32[25,16384]{1,0:T(8,128)S(1)} %bitcast.308), kind=kOutput, calls=%fused_computation.11 | convolution fusion | flops 122880000 | bytes 3279300 | tf_op jit(solution)/shard_map/vbp,cp->vbc/dot_general | solution.py:111
  110.7 2.5 %fusion.137 = f32[1,25]{1,0:T(1,128)} fusion(f32[16384,1]{0,1:T(1,128)S(1)} %bitcast.325, f32[25,16384]{1,0:T(8,128)S(1)} %bitcast.309), kind=kOutput, calls=%fused_computation.205 | convolution fusion | flops 4915200 | bytes 1704036 | tf_op jit(solution)/shard_map/cp,vp->vc/dot_general | solution.py:112
  113.2 0.3 pad.19
  113.5 1.2 copy.31
  114.7 1.2 copy.32
  116.0 2.4 %convolution_bitcast_fusion.2 = f32[1,25,25]{1,2,0:T(8,128)} fusion(f32[25,16384]{1,0:T(8,128)S(1)} %bitcast.319, f32[25,16384]{1,0:T(8,128)S(1)} %bitcast.310), kind=kOutput, calls=%fused_computation.10 | convolution fusion | flops 122880000 | bytes 3279300 | tf_op jit(solution)/shard_map/vbp,cp->vbc/dot_general | solution.py:111
  118.4 2.3 %fusion.138 = f32[1,25]{1,0:T(1,128)} fusion(f32[16384,1]{0,1:T(1,128)S(1)} %bitcast.324, f32[25,16384]{1,0:T(8,128)S(1)} %bitcast.311), kind=kOutput, calls=%fused_computation.206 | convolution fusion | flops 4915200 | bytes 1704036 | tf_op jit(solution)/shard_map/cp,vp->vc/dot_general | solution.py:112
  120.7 14.6 %all-reduce.3 = (f32[1,25,25]{1,2,0:T(8,128)}, f32[1,25]{1,0:T(1,128)}, f32[1,25,25]{1,2,0:T(8,128)}, f32[1,25]{1,0:T(1,128)}) all-reduce(f32[1,25,25]{1,2,0:T(8,128)} %convolution_bitcast_fusion.2, f32[1,25]{1,0:T(1,128)} %fusion.138, f32[1,25,25]{1,2,0:T(8,128)S(1)} %convolution_bitcast_fusion.3, ...), channel_id=1, replica_groups=mesh['visit'=8,'patch'=4] {'patch'}, use_global_device_ids=true, to_apply=%region_6.9 | all-reduce | flops 1300 | bytes 10400 | tf_op jit(solution)/shard_map/psum | solution.py:118
  135.3 1.3 convert_add_fusion
  136.6 0.8 copy.17
  137.4 1.3 fusion.86
  138.8 3.0 %custom-call.12 = f32[1,25,25]{2,1,0:T(8,128)S(1)} custom-call(f32[1,25,25]{2,1,0:T(8,128)} %fusion.86), custom_call_target="Cholesky" | custom-call | tf_op jit(solution)/shard_map/vmap(jit(cholesky))/cholesky | solution.py:83
  141.8 0.6 compare_reduce_fusion
  142.4 1.2 fusion.83
  143.6 2.6 %custom-call.13 = f32[1,1,25,25]{2,3,1,0:T(8,128)S(1)} custom-call(f32[1,1,25,25]{3,2,1,0:T(8,128)} %fusion.83), custom_call_target="InvertDiagBlocksLowerTriangular" | custom-call | tf_op jit(solution)/shard_map/vmap(jit(_cho_solve))/triangular_solve | solution.py:84
  146.2 0.8 convolution_bitcast_fusion.5
  147.0 0.6 convolution_bitcast_fusion.4
  147.7 1.3 convert_add_fusion.1
  149.0 0.8 copy.14
  149.8 1.3 fusion.89
  151.1 3.0 %custom-call.10 = f32[1,25,25]{2,1,0:T(8,128)S(1)} custom-call(f32[1,25,25]{2,1,0:T(8,128)} %fusion.89), custom_call_target="Cholesky" | custom-call | tf_op jit(solution)/shard_map/vmap(jit(cholesky))/cholesky | solution.py:83
  154.1 0.7 compare_reduce_fusion.1
  154.8 1.2 fusion.82
  156.1 2.6 %custom-call.11 = f32[1,1,25,25]{2,3,1,0:T(8,128)S(1)} custom-call(f32[1,1,25,25]{3,2,1,0:T(8,128)} %fusion.82), custom_call_target="InvertDiagBlocksLowerTriangular" | custom-call | tf_op jit(solution)/shard_map/vmap(jit(_cho_solve))/triangular_solve | solution.py:84
  158.7 0.8 convolution_bitcast_fusion.7
  159.5 0.1 convolution_bitcast_fusion.6
  159.7 2.6 %fusion = f32[1,16,1024]{2,0,1:T(1,128)S(1)} fusion(f32[25,1,1]{0,1,2:T(1,128)} %convolution_bitcast_fusion.4, f32[16,1024,25]{1,0,2:T(8,128)S(1)} %slice_bitcast_fusion), kind=kOutput, calls=%fused_computation | convolution fusion | flops 4915200 | bytes 1704036 | tf_op jit(solution)/shard_map/vb,bp->vp/dot_general | solution.py:89
  162.3 2.0 %fusion.2 = f32[1,16,1024]{2,0,1:T(1,128)S(1)} fusion(f32[25,1,1]{0,1,2:T(1,128)S(1)} %convolution_bitcast_fusion.6, f32[16,1024,25]{1,0,2:T(8,128)S(1)} %slice_bitcast_fusion.1), kind=kOutput, calls=%fused_computation.2 | convolution fusion | flops 4915200 | bytes 1704036 | tf_op jit(solution)/shard_map/vb,bp->vp/dot_general | solution.py:89
  164.4 0.7 pad_maximum_fusion.2
  (100 shorter events, 1.6 us)
Async XLA Ops:
  6.5 5.0 %copy-start.8 = (f32[5]{0:T(128)S(1)}, f32[5]{0:T(128)}, u32[]{:S(2)}) copy-start(f32[5]{0:T(128)} %constant.163) | copy-start | bytes 64
  6.5 5.0 %copy-start.9 = (f32[5]{0:T(128)S(1)}, f32[5]{0:T(128)}, u32[]{:S(2)}) copy-start(f32[5]{0:T(128)} %constant.161) | copy-start | bytes 64
  6.5 5.0 %copy-start.10 = (f32[5]{0:T(128)S(1)}, f32[5]{0:T(128)}, u32[]{:S(2)}) copy-start(f32[5]{0:T(128)} %constant.159) | copy-start | bytes 64
  6.5 5.1 %copy-start.11 = (f32[5]{0:T(128)S(1)}, f32[5]{0:T(128)}, u32[]{:S(2)}) copy-start(f32[5]{0:T(128)} %constant.157) | copy-start | bytes 64
  6.5 5.1 %copy-start.12 = (f32[5]{0:T(128)S(1)}, f32[5]{0:T(128)}, u32[]{:S(2)}) copy-start(f32[5]{0:T(128)} %constant.155) | copy-start | bytes 64
  6.6 5.1 %copy-start.13 = (f32[5]{0:T(128)S(1)}, f32[5]{0:T(128)}, u32[]{:S(2)}) copy-start(f32[5]{0:T(128)} %constant.153) | copy-start | bytes 64
  6.6 5.1 %copy-start.14 = (f32[5]{0:T(128)S(1)}, f32[5]{0:T(128)}, u32[]{:S(2)}) copy-start(f32[5]{0:T(128)} %constant.151) | copy-start | bytes 64
  6.6 5.1 %copy-start.15 = (f32[5]{0:T(128)S(1)}, f32[5]{0:T(128)}, u32[]{:S(2)}) copy-start(f32[5]{0:T(128)} %constant.149) | copy-start | bytes 64
  6.6 5.1 %copy-start.16 = (f32[5]{0:T(128)S(1)}, f32[5]{0:T(128)}, u32[]{:S(2)}) copy-start(f32[5]{0:T(128)} %constant.147) | copy-start | bytes 64
  6.6 5.1 %copy-start.17 = (f32[5]{0:T(128)S(1)}, f32[5]{0:T(128)}, u32[]{:S(2)}) copy-start(f32[5]{0:T(128)} %constant.145) | copy-start | bytes 64
  6.6 5.1 %copy-start.18 = (f32[5]{0:T(128)S(1)}, f32[5]{0:T(128)}, u32[]{:S(2)}) copy-start(f32[5]{0:T(128)} %constant.143) | copy-start | bytes 64
  6.6 5.1 %copy-start.19 = (f32[5]{0:T(128)S(1)}, f32[5]{0:T(128)}, u32[]{:S(2)}) copy-start(f32[5]{0:T(128)} %constant.141) | copy-start | bytes 64
  6.6 5.0 %copy-start.20 = (f32[5]{0:T(128)S(1)}, f32[5]{0:T(128)}, u32[]{:S(2)}) copy-start(f32[5]{0:T(128)} %constant.139) | copy-start | bytes 64
  6.7 5.0 %copy-start.21 = (f32[5]{0:T(128)S(1)}, f32[5]{0:T(128)}, u32[]{:S(2)}) copy-start(f32[5]{0:T(128)} %constant.137) | copy-start | bytes 64
  6.7 5.0 %copy-start.22 = (f32[5]{0:T(128)S(1)}, f32[5]{0:T(128)}, u32[]{:S(2)}) copy-start(f32[5]{0:T(128)} %constant.135) | copy-start | bytes 64
  6.7 5.0 %copy-start.23 = (f32[5]{0:T(128)S(1)}, f32[5]{0:T(128)}, u32[]{:S(2)}) copy-start(f32[5]{0:T(128)} %constant.133) | copy-start | bytes 64
  6.7 5.0 %copy-start.24 = (f32[5]{0:T(128)S(1)}, f32[5]{0:T(128)}, u32[]{:S(2)}) copy-start(f32[5]{0:T(128)} %constant.131) | copy-start | bytes 64
  6.7 5.0 %copy-start.25 = (f32[5]{0:T(128)S(1)}, f32[5]{0:T(128)}, u32[]{:S(2)}) copy-start(f32[5]{0:T(128)} %constant.129) | copy-start | bytes 64
  6.7 5.0 %copy-start.26 = (f32[5]{0:T(128)S(1)}, f32[5]{0:T(128)}, u32[]{:S(2)}) copy-start(f32[5]{0:T(128)} %constant.127) | copy-start | bytes 64
  6.7 5.0 %copy-start.27 = (f32[5]{0:T(128)S(1)}, f32[5]{0:T(128)}, u32[]{:S(2)}) copy-start(f32[5]{0:T(128)} %constant.125) | copy-start | bytes 64
  6.7 5.0 %copy-start.28 = (f32[5]{0:T(128)S(1)}, f32[5]{0:T(128)}, u32[]{:S(2)}) copy-start(f32[5]{0:T(128)} %constant.123) | copy-start | bytes 64
  6.8 78.0 %all-reduce.6.cloned.1.call-start = ((), (), s32[]{:S(2)}) async-start(), calls=%async_computation | async-start | bytes 524288 | tf_op jit(solution)/shard_map/psum | solution.py:17
  11.3 84.0 %copy-start.2 = (f32[2,1,16,1024]{3,2,1,0:T(8,128)S(1)}, f32[2,1,16,1024]{3,2,1,0:T(8,128)}, u32[]{:S(2)}) copy-start(f32[2,1,16,1024]{3,2,1,0:T(8,128)} %param.12) | copy-start | bytes 393220
  11.3 84.0 %copy-start.3 = (f32[2,1,16,1024]{3,2,1,0:T(8,128)S(1)}, f32[2,1,16,1024]{3,2,1,0:T(8,128)}, u32[]{:S(2)}) copy-start(f32[2,1,16,1024]{3,2,1,0:T(8,128)} %param.13) | copy-start | bytes 393220
  11.3 84.0 %copy-start.4 = (s32[2,1,16,1024]{3,2,1,0:T(8,128)S(1)}, s32[2,1,16,1024]{3,2,1,0:T(8,128)}, u32[]{:S(2)}) copy-start(s32[2,1,16,1024]{3,2,1,0:T(8,128)} %param.14) | copy-start | bytes 393220
  85.7 12.0 %collective-permute-start.2 = (f32[10,1024]{1,0:T(8,128)S(1)}, f32[10,1024]{1,0:T(8,128)S(1)}, u32[]{:S(2)}, u32[]{:S(2)}) collective-permute-start(f32[10,1024]{1,0:T(8,128)S(1)} %get-tuple-element.23), channel_id=1, source_target_pairs={{0,1},{1,2},{2,3},{4,5},{5,6},{6,7},{8,9},{9,10},{10,11},{12,13},{... | collective-permute-start | bytes 122888 | tf_op jit(solution)/shard_map/ppermute | solution.py:28
  87.0 10.7 %collective-permute-start.3 = (f32[10,1024]{1,0:T(8,128)S(1)}, f32[10,1024]{1,0:T(8,128)S(1)}, u32[]{:S(2)}, u32[]{:S(2)}) collective-permute-start(f32[10,1024]{1,0:T(8,128)S(1)} %get-tuple-element.24), channel_id=1, source_target_pairs={{1,0},{2,1},{3,2},{5,4},{6,5},{7,6},{9,8},{10,9},{11,10},{13,12},{... | collective-permute-start | bytes 122888 | tf_op jit(solution)/shard_map/ppermute | solution.py:30
  89.3 8.5 %collective-permute-start = (f32[10,1024]{1,0:T(8,128)S(1)}, f32[10,1024]{1,0:T(8,128)S(1)}, u32[]{:S(2)}, u32[]{:S(2)}) collective-permute-start(f32[10,1024]{1,0:T(8,128)S(1)} %get-tuple-element.21), channel_id=1, source_target_pairs={{0,1},{1,2},{2,3},{4,5},{5,6},{6,7},{8,9},{9,10},{10,11},{12,13},{... | collective-permute-start | bytes 122888 | tf_op jit(solution)/shard_map/ppermute | solution.py:28
  94.0 4.4 %collective-permute-start.1 = (f32[10,1024]{1,0:T(8,128)S(1)}, f32[10,1024]{1,0:T(8,128)S(1)}, u32[]{:S(2)}, u32[]{:S(2)}) collective-permute-start(f32[10,1024]{1,0:T(8,128)S(1)} %get-tuple-element.22), channel_id=1, source_target_pairs={{1,0},{2,1},{3,2},{5,4},{6,5},{7,6},{9,8},{10,9},{11,10},{13,12},{... | collective-permute-start | bytes 122888 | tf_op jit(solution)/shard_map/ppermute | solution.py:30
  108.9 1.9 %copy-start.7 = (f32[1,1,16,1024]{3,1,2,0:T(1,128)S(1)}, f32[1,1,16,1024]{3,1,2,0:T(1,128)}, u32[]{:S(2)}) copy-start(f32[1,1,16,1024]{3,1,2,0:T(1,128)} %copy.29) | copy-start | bytes 196612
  115.9 2.5 %copy-start.6 = (f32[1,1,16,1024]{3,1,2,0:T(1,128)S(1)}, f32[1,1,16,1024]{3,1,2,0:T(1,128)}, u32[]{:S(2)}) copy-start(f32[1,1,16,1024]{3,1,2,0:T(1,128)} %copy.33) | copy-start | bytes 196612
  159.7 4.6 %copy-start = (f32[2,16,1024]{2,1,0:T(8,128)S(1)}, f32[2,16,1024]{2,1,0:T(8,128)}, u32[]{:S(2)}) copy-start(f32[2,16,1024]{2,1,0:T(8,128)} %get-tuple-element.6) | copy-start | bytes 393220
  159.7 4.6 %copy-start.1 = (f32[2,16,1024]{2,1,0:T(8,128)S(1)}, f32[2,16,1024]{2,1,0:T(8,128)}, u32[]{:S(2)}) copy-start(f32[2,16,1024]{2,1,0:T(8,128)} %get-tuple-element.8) | copy-start | bytes 393220
  159.7 4.6 %copy-start.5 = (s32[2,1,16,1024]{3,2,1,0:T(8,128)S(1)}, s32[2,1,16,1024]{3,2,1,0:T(8,128)}, u32[]{:S(2)}) copy-start(s32[2,1,16,1024]{3,2,1,0:T(8,128)} %param.14) | copy-start | bytes 393220
Sparse Core Ops, SparseCore 0:
  11.2 73.5 all-reduce.5
where the time goes:
time: 173 us; the launch traced here: 172 us
  waiting for transfers between devices  72.8 us (42%)
  other arithmetic  24.9 us (14%)
  matrix products  21.2 us (12%)
  between operations  15.5 us (9%)
  blocking collectives  14.6 us (8%)
  local copies, waits for them, and re-layouts  14.3 us (8%)
  starting transfers between devices  8.66 us (5%)
    psum x1, waiting for transfers between devices, from_root(): return lax.psum(block, axis)  72.1 us
    psum x1, blocking collectives, shards(): summed_mat, summed_rhs = lax.psum((normal_mat, normal_rhs), 'patch')  14.6 us
    unnamed x82, local copies, waits for them, and re-layouts  8.57 us
    another operation x4, other arithmetic, solve_kernel(): return jax.scipy.linalg.cho_solve((factor, True), normal_rhs)  7.65 us
    another operation x6, other arithmetic, solve_kernel(): jnp.linalg.cholesky(normal_mat + ridge * jnp.eye(count, dtype=jnp.float32))  7.36 us
    ppermute x2, starting transfers between devices, padded(): lax.ppermute(tail, axis, [(i, (i + 1) % count) for i in range(ends)])  6.03 us
    dot_general x2, matrix products, shards(): jnp.einsum('cp,vp->vc', flattened, (weight * science[current]).reshape(vi...  4.8 us
    dot_general x2, matrix products, finish_step(): jnp.einsum('vb,bp->vp', kernel_coef, flattened, precision=lax.Precision.H...  4.58 us
  transfers between devices with their start and end apart: 5, of which 2 were waited for; matrix products, arithmetic and copies ran while one was open for 3% of the time, Pallas kernels for 0%

commit v1 on v0

v1 whole, which is shorter than its diff:
```python
import jax
import jax.numpy as jnp
import numpy as np
from jax import lax
from jax.experimental import pallas as pl
from jax.experimental.pallas import tpu as pltpu
from jax.sharding import PartitionSpec as P

NPROF = 5
RAD = 10
STEPS = 2
SUB = 8
LANE = 128

GROUPS = NPROF - 1
STACK = GROUPS * SUB
SPARE = SUB - NPROF
SCI_ROW = 2 * SUB + NPROF
SPOTS = [i * SUB + j for i in range(GROUPS) for j in range(NPROF)]
SPOTS += [(j // SPARE) * SUB + NPROF + j % SPARE for j in range(NPROF)]

PIVOTS = 9

PIECES = 2

FIRST_CHUNK, SECOND_CHUNK = 2 * LANE, 4 * LANE

ridge = 1.0


def profile_table():
    offsets = np.arange(-RAD, RAD + 1) * 1.0
    recipe = [(1.0, 0), (1.5, 1), (2.0, 2), (3.0, 0), (4.0, 1)]
    profiles = []
    for spread, degree in recipe[:NPROF]:
        profile = offsets**degree * np.exp(-offsets * offsets / (2.0 * spread * spread))
        for earlier in profiles:
            profile = profile - np.dot(earlier, profile) * earlier
        profile = profile / np.sqrt(np.dot(profile, profile))
        profiles.append(profile)
    return np.stack(profiles)


PARITY = [0, 1, 0, 0, 1]


def split_bf16(x, parts):
    pieces = []
    for _ in range(parts - 1):
        piece = x.astype(jnp.bfloat16).astype(jnp.float32)
        pieces.append(piece)
        x = x - piece
    return pieces + [x]


EXTRA = RAD % SUB
SLOTS = SUB // EXTRA


def vertical_table(rows):
    profiles = profile_table()
    near = RAD - EXTRA
    blank = [None] * (SUB - EXTRA)
    own = list(range(rows))
    above = [list(range(-near, 0)), list(range(-RAD, -near)) + blank]
    below = [list(range(rows, rows + near)), list(range(rows + near, rows + RAD)) + blank]
    both = []
    for inside, across, shift in ((below, above, RAD), (above, below, 0)):
        order = [(k + shift) % rows for k in range(rows)]
        joined = []
        for outputs, blocks in ((order, [own] + inside), (order[rows - RAD :], across)):
            tables = []
            for block in blocks:
                table = np.zeros((len(outputs) * SUB, len(block)), np.float32)
                for n, r in enumerate(outputs):
                    for j in range(NPROF):
                        for e, offset in enumerate(block):
                            if offset is not None and abs(offset - r) <= RAD:
                                table[n * SUB + j, e] = profiles[j, offset - r + RAD]
                hi = table.astype(jnp.bfloat16).astype(np.float32)
                mid = (table - hi).astype(jnp.bfloat16).astype(np.float32)
                low = table - hi - mid
                tables += [hi, hi, mid, hi, mid, low]
            joined.append(np.concatenate(tables, axis=1))
        width = max(table.shape[1] for table in joined)
        joined = [np.pad(table, ((0, 0), (0, width - table.shape[1]))) for table in joined]
        both.append(np.concatenate(joined, axis=0))
    return jnp.asarray(np.stack(both), jnp.bfloat16)


def patch_parity():
    return lax.rem(lax.axis_index("patch"), 2)


def six_products(hi, mid, low):
    return [hi, mid, hi, low, mid, hi]


def vmem_specs(count):
    return [pl.BlockSpec(memory_space=pltpu.VMEM)] * count


def grant(mebibytes):
    return pltpu.CompilerParams(vmem_limit_bytes=mebibytes * 1024 * 1024)


def estimate(operations):
    return pl.CostEstimate(flops=operations, bytes_accessed=1024 * 1024, transcendentals=0)


def pick_kernel(visits, per, owners, science, table, got, out):
    turn = (visits // 2) * patch_parity()
    for s in range(STEPS):
        place = lax.rem(owners[s] + turn, jnp.full((SUB, LANE), visits))
        for n in range(per):
            chosen = got[n]
            for v in range(1, visits):
                chosen = jnp.where(place == v, got[v * per + n], chosen)
            for v in range(visits):
                out[v, s, n] = chosen


def exchange(blocks):
    visits, patches = lax.axis_size("visit"), lax.axis_size("patch")
    groups = [
        [(n + (visits // 2) * (p % 2)) % visits * patches + p for n in range(visits)]
        for p in range(patches)
    ]
    return lax.all_to_all(
        blocks, ("visit", "patch"), 0, 0, axis_index_groups=groups, tiled=True
    )


def choose_owned(own, owners, science, table):
    visits = lax.axis_size("visit")
    shape = own.shape
    rows, cols = shape[-2:]
    tiles = own.reshape(shape[0], rows // SUB, SUB, cols // LANE, LANE)
    tiles = jnp.transpose(tiles, (0, 1, 3, 2, 4)).reshape(-1, SUB, LANE)
    per = tiles.shape[0] // visits
    got = exchange(tiles)

    def pick(*refs):
        pick_kernel(visits, per, *refs)

    return pl.pallas_call(
        pick,
        out_shape=jax.ShapeDtypeStruct((visits, STEPS, per, SUB, LANE), jnp.float32),
        in_specs=vmem_specs(1) + [pl.BlockSpec(memory_space=pl.ANY)] * 2 + vmem_specs(1),
        out_specs=vmem_specs(1)[0],
        compiler_params=grant(8),
    )(owners, science, table, got)


def stage_kernel(owners_in, table_in, owners, table):
    owners[...] = owners_in[...]
    table[...] = table_in[...]


def row_cells(ref, s, image, row_tile, shape):
    rows, cols, per = shape
    start = (image * (rows // SUB) + row_tile) * (cols // LANE)
    found = [ref[t // per, s, t % per] for t in range(start, start + cols // LANE)]
    return jnp.concatenate(found, axis=1)


def columns_in_parts(piece):
    profiles = profile_table()
    cols = piece.shape[1]
    width = cols + LANE
    wide = jnp.concatenate([piece, jnp.zeros((SUB, LANE), jnp.float32)], axis=1)
    totals = [piece * float(profiles[i, RAD]) if PARITY[i] == 0 else None for i in range(NPROF)]
    for d in range(1, RAD + 1):
        ahead = pltpu.roll(wide, width - d, 1)[:, :cols]
        behind = pltpu.roll(wide, d, 1)[:, :cols]
        both = (ahead + behind, ahead - behind)
        for i in range(NPROF):
            term = both[PARITY[i]] * float(profiles[i, RAD + d])
            totals[i] = term if totals[i] is None else totals[i] + term
        yield
    return totals


def advance(parts, count=None):
    while count is None or count > 0:
        try:
            next(parts)
        except StopIteration as stop:
            return stop.value
        count = None if count is None else count - 1
    return None


def along_columns(piece):
    return advance(columns_in_parts(piece))


def pass_own_rows(shape, parity, arrived, science_in, signed_var, columns, weights, scale, science):
    rows, cols, _ = shape
    row_tiles = rows // SUB
    sub = lax.broadcasted_iota(jnp.int32, (SUB, cols), 0)

    def put(ref, s, tiles):
        if parity == 0:
            moved = [pltpu.roll(tile, SUB - RAD % SUB, 0) for tile in tiles]
            tiles = []
            for t in range(row_tiles):
                near = (t + RAD // SUB) % row_tiles
                far = (near + 1) % row_tiles
                tiles.append(jnp.where(sub < SUB - RAD % SUB, moved[near], moved[far]))
        for t, tile in enumerate(tiles):
            ref[s, t * SUB : (t + 1) * SUB, :] = tile

    for s in range(STEPS):
        found = [along_columns(row_cells(arrived, s, 0, t, shape)) for t in range(row_tiles)]
        for i in range(NPROF):
            column = jnp.concatenate([piece[i] for piece in found], axis=0)
            for n, piece in enumerate(split_bf16(column, 3)):
                columns[s, i, n] = piece.astype(jnp.bfloat16)
        found = []
        for t in range(row_tiles):
            here = slice(t * SUB, (t + 1) * SUB)
            sci_var = signed_var[s, 0, here, :]
            usable = jnp.where(sci_var > 0.0, 1.0, 0.0)
            noise_var = jnp.abs(sci_var) + row_cells(arrived, s, 1, t, shape)
            found.append(usable / noise_var)
            scale[s, here, :] = usable * lax.rsqrt(noise_var)
        put(weights, s, found)
        put(science, s, [science_in[s, 0, t * SUB : (t + 1) * SUB, :] for t in range(row_tiles)])


def pack_kernel(shape, arrived, science, signed_var, across, inside, *own):
    rows, cols, _ = shape
    last = rows // SUB - 1
    col_tiles = cols // LANE
    odd = jnp.full((SUB, LANE), patch_parity()) == 1
    slot = lax.broadcasted_iota(jnp.int32, (SUB, LANE), 0) // EXTRA
    for s in range(STEPS):
        cells = [row_cells(arrived, s, 0, t, shape) for t in (0, 1, last - 1, last)]
        for group in range(col_tiles // SLOTS):
            tail, head = None, None
            for q in range(SLOTS):
                c = group * SLOTS + q
                there = slice(c * LANE, (c + 1) * LANE)
                first, second, before, final = (cell[:, there] for cell in cells)
                across[s, c] = jnp.where(odd, final, first)
                inside[s, c] = jnp.where(odd, first, final)
                low = pltpu.roll(before, (q + 1) * EXTRA, 0)
                high = pltpu.roll(second, q * EXTRA, 0)
                tail = low if tail is None else jnp.where(slot == q, low, tail)
                head = high if head is None else jnp.where(slot == q, high, head)
            across[s, col_tiles + group] = jnp.where(odd, tail, head)
            inside[s, col_tiles + group] = jnp.where(odd, head, tail)

    @pl.when(patch_parity() == 1)
    def _():
        pass_own_rows(shape, 1, arrived, science, signed_var, *own)


def own_kernel(shape, arrived, science, signed_var, *refs):
    @pl.when(patch_parity() == 0)
    def _():
        pass_own_rows(shape, 0, arrived, science, signed_var, *refs[len(refs) // 2 :])


def near_columns(halo, s, cols):
    return columns_in_parts(jnp.concatenate([halo[s, c] for c in range(cols // LANE)], axis=1))


def extra_columns(halo, cols):
    sub = lax.broadcasted_iota(jnp.int32, (SUB, LANE), 0)
    col_tiles = cols // LANE
    extra = []
    for c in range(col_tiles):
        found = None
        for s in range(STEPS):
            moved = pltpu.roll(
                halo[s, col_tiles + c // SLOTS], (SUB + (s - c % SLOTS) * EXTRA) % SUB, 0
            )
            found = moved if found is None else jnp.where(sub < s * EXTRA, found, moved)
        extra.append(found)
    extra = along_columns(jnp.concatenate(extra, axis=1))
    return [[pltpu.roll(x, SUB - s * EXTRA, 0) if s else x for x in extra] for s in range(STEPS)]


def split_tile(tile):
    return jnp.concatenate(six_products(*split_bf16(tile, 3)), axis=0).astype(jnp.bfloat16)


def fit_rows(s, first, count, there, images, weights, science, stack):
    sub = lax.broadcasted_iota(jnp.int32, (SUB, there.stop - there.start), 0)
    total = None
    for n in range(count):
        k = first + n
        here = slice(n * SUB, (n + 1) * SUB)
        last = images[GROUPS][here, :]
        groups = []
        for i in range(GROUPS):
            found = images[i][here, :]
            if i < 2:
                turn = (NPROF - i * SPARE) % SUB
                found = jnp.where(sub < NPROF, found, pltpu.roll(last, turn, 0))
            elif i == 2:
                found = jnp.where(sub == NPROF, science[s, k : k + 1, there], found)
            stack[s, n, i * SUB : (i + 1) * SUB, there] = found
            groups.append(found)
        found = jnp.concatenate(groups, axis=0)
        hi = found.astype(jnp.bfloat16)
        mid = (found - hi.astype(jnp.float32)).astype(jnp.bfloat16)
        rounded = (found * weights[s, k : k + 1, there]).astype(jnp.bfloat16)
        product = lax.dot_general(
            jnp.concatenate([rounded, rounded], axis=1),
            jnp.concatenate([hi, mid], axis=1),
            (((1,), (1,)), ((), ())),
            preferred_element_type=jnp.float32,
        )
        total = product if total is None else total + product
    return total


def fit_chunks(halo, cols, chunk, first, count, vertical, weights, science, stack):
    extra = extra_columns(halo, cols)
    near = advance(near_columns(halo, 0, cols))
    starts = range(0, cols, chunk)
    items = [(s, slice(start, start + chunk)) for s in range(STEPS) for start in starts]
    images = vertical(0, items[0][1], near, extra[0])
    totals = [None] * STEPS
    coming = None
    for n, (s, there) in enumerate(items):
        following = items[n + 1] if n + 1 < len(items) else None
        if following is not None:
            if s + 1 < STEPS:
                if coming is None:
                    coming, found = near_columns(halo, s + 1, cols), None
                share = None if following[0] != s else -(-RAD // (len(starts) - 1))
                found = advance(coming, share) if found is None else found
            if following[0] != s:
                near, coming = found, None
            upcoming = vertical(*following, near, extra[following[0]])
        total = fit_rows(s, first, count, there, images, weights, science, stack)
        totals[s] = total if totals[s] is None else totals[s] + total
        images = upcoming if following is not None else None
    sides = []
    for total in totals:
        sides.append(total)
        sides.append(jnp.zeros((STACK, LANE // STEPS - STACK), jnp.float32))
    return jnp.concatenate(sides, axis=1)


def first_kernel(shape, inside, own, weights, science, table, normal, stack, partial):
    rows, cols, _ = shape
    early = rows - RAD

    def vertical(s, there, near, extra):
        images = []
        for i in range(NPROF):
            spread = six_products(*(own[s, i, n, :, there] for n in range(3)))
            spread += [split_tile(near[i][:, there]), split_tile(extra[i][:, there])]
            image = jnp.dot(
                table[patch_parity(), : rows * SUB, :],
                jnp.concatenate(spread, axis=0),
                preferred_element_type=jnp.float32,
            )
            images.append(image[: early * SUB, :])
            partial[s, i, :, there] = image[early * SUB :, :]
        return images

    normal[...] = fit_chunks(inside, cols, FIRST_CHUNK, 0, early, vertical, weights, science, stack)


def second_kernel(shape, across, weights, science, table, before, partial, normal, stack):
    rows, cols, _ = shape

    def vertical(s, there, near, extra):
        images = []
        for i in range(NPROF):
            spread = [split_tile(near[i][:, there]), split_tile(extra[i][:, there])]
            spread = jnp.concatenate(spread, axis=0)
            image = jnp.dot(
                table[patch_parity(), rows * SUB :, : spread.shape[0]],
                spread,
                preferred_element_type=jnp.float32,
            )
            images.append(partial[s, i, :, there] + image)
        return images

    found = fit_chunks(
        across, cols, SECOND_CHUNK, rows - RAD, RAD, vertical, weights, science, stack
    )
    normal[...] = before[...] + found


def solve_both(blocks):
    half = LANE // STEPS
    sub = lax.broadcasted_iota(jnp.int32, (SUB, LANE), 0)
    lane = lax.broadcasted_iota(jnp.int32, (SUB, LANE), 1)

    def spread(k):
        return [
            jnp.where(lane < half, block[:, k : k + 1], block[:, half + k : half + k + 1])
            for block in blocks
        ]

    def entry(column, k):
        row = column[k // SUB][k % SUB : k % SUB + 1, :]
        return jnp.broadcast_to(row, (SUB, LANE))

    for start in range(0, len(SPOTS), PIVOTS):
        spots = SPOTS[start : start + PIVOTS]
        columns = [spread(k) for k in spots]
        inner = [[entry(column, k) for column in columns] for k in spots]
        rows = [entry(blocks, k) for k in spots]
        for t in range(len(spots)):
            inverse = 1.0 / inner[t][t]
            inner[t] = [x * inverse for x in inner[t]]
            rows[t] = rows[t] * inverse
            for n in range(len(spots)):
                if n != t:
                    factor = inner[n][t]
                    inner[n] = [x - factor * y for x, y in zip(inner[n], inner[t])]
                    rows[n] = rows[n] - factor * rows[t]
        updated = []
        for i, block in enumerate(blocks):
            terms = [column[i] * row for column, row in zip(columns, rows)]
            while len(terms) > 1:
                terms = [sum(terms[n : n + 2][1:], terms[n]) for n in range(0, len(terms), 2)]
            block = block - terms[0]
            for k, row in zip(spots, rows):
                if k // SUB == i:
                    block = jnp.where(sub == k % SUB, row, block)
            updated.append(block)
        blocks = updated
    return blocks


def fold_rows(found):
    sub = lax.broadcasted_iota(jnp.int32, found[0].shape, 0)
    hop = SUB // 2
    while hop:
        upper = (sub & hop) != 0
        count = len(found) // 2
        joined = []
        for low, high in zip(found[:count], found[count:]):
            kept = jnp.where(upper, high, low)
            if 2 * hop == SUB:
                moved = pltpu.roll(jnp.where(upper, low, high), hop, 0)
            else:
                moved = jnp.where(
                    upper, pltpu.roll(high, hop, 0), pltpu.roll(low, SUB - hop, 0)
                )
            joined.append(kept + moved)
        found = joined
        hop //= 2
    return found[0]


def solve_kernel(rows, cols, count, *refs):
    parts, (scale, early, late, out, held, sems) = refs[:count], refs[count:]
    copies = []
    odd = jnp.full((SUB, LANE), patch_parity()) == 1
    turn = rows - RAD
    half = LANE // STEPS
    sub = lax.broadcasted_iota(jnp.int32, (SUB, LANE), 0)
    lane = lax.broadcasted_iota(jnp.int32, (SUB, LANE), 1)
    blocks = []
    for start in range(0, STACK, SUB):
        block = jnp.where(lax.rem(lane, half) == sub + start, ridge, 0.0)
        for part in parts:
            block = block + part[start : start + SUB, :]
        blocks.append(block)
    solved = solve_both(blocks)
    for s in range(STEPS):
        factors = []
        for i in range(GROUPS):
            spot = s * half + SCI_ROW
            factor = jnp.broadcast_to(solved[i][:, spot : spot + 1], (SUB, LANE))
            used = [k % SUB for k in SPOTS if k // SUB == i]
            if len(used) < SUB:
                factor = jnp.where(sub < len(used), factor, 0.0)
            if i == SCI_ROW // SUB:
                factor = jnp.where(sub == SCI_ROW % SUB, -1.0, factor)
            factors.append(factor)
        for c in range(cols // LANE):
            there = slice(c * LANE, (c + 1) * LANE)
            found = []
            for k in range(rows):
                source, n = (early, k) if k < turn else (late, k - turn)
                total = source[s, n, 0:SUB, there] * factors[0]
                for i in range(1, GROUPS):
                    total = total + source[s, n, i * SUB : (i + 1) * SUB, there] * factors[i]
                found.append(total)
            tiles = [fold_rows(found[k : k + SUB]) for k in range(0, rows, SUB)]
            moved = [pltpu.roll(tile, (SUB - turn) % SUB, 0) for tile in tiles]
            for t, tile in enumerate(tiles):
                after = (t + turn // SUB) % len(tiles)
                ahead = (after + 1) % len(tiles)
                turned = jnp.where(sub < SUB - turn % SUB, moved[after], moved[ahead])
                here = slice(t * SUB, (t + 1) * SUB)
                left = jnp.where(odd, tile, turned)
                held[s, 0, here, there] = -left * scale[s, here, there]
            if there.stop % (cols // PIECES) == 0:
                whole = (s, slice(None), slice(None), pl.ds(there.stop - cols // PIECES, cols // PIECES))
                copy = pltpu.make_async_copy(held.at[whole], out.at[whole], sems.at[len(copies)])
                copy.start()
                copies.append(copy)
    for copy in copies:
        copy.wait()


def shards(templates, owners, science, sci_var, bad_pixels):
    rows, cols = templates.shape[-2:]
    image = jax.ShapeDtypeStruct((STEPS, rows, cols), jnp.float32)
    held = jax.ShapeDtypeStruct(science.shape, jnp.float32)
    bad = bad_pixels != 0
    science = jnp.where(bad, 0.0, science)
    signed_var = jnp.where(bad, -sci_var, sci_var)
    table = vertical_table(rows)
    owners = jnp.broadcast_to(owners[:, None, None], (STEPS, SUB, LANE))
    owners, table = pl.pallas_call(
        stage_kernel,
        out_shape=[jax.ShapeDtypeStruct(x.shape, x.dtype) for x in (owners, table)],
        in_specs=vmem_specs(2),
        out_specs=vmem_specs(2),
        compiler_params=grant(8),
        cost_estimate=estimate(1 << 20),
    )(owners, table)
    chosen = choose_owned(templates[0], owners, science, table)
    arrived = exchange(chosen)
    visits, per = arrived.shape[0], arrived.shape[2]
    shape = (rows, cols, per)

    own_shapes = (
        jax.ShapeDtypeStruct((STEPS, NPROF, 3, rows, cols), jnp.bfloat16),
        image,
        image,
        image,
    )

    def pack(*refs):
        pack_kernel(shape, *refs)

    tiles = cols // LANE
    packed = jax.ShapeDtypeStruct((STEPS, tiles + tiles // SLOTS, SUB, LANE), jnp.float32)
    across, inside, *own = pl.pallas_call(
        pack,
        out_shape=(packed, packed) + own_shapes,
        in_specs=vmem_specs(3),
        out_specs=vmem_specs(6),
        compiler_params=grant(8),
    )(arrived, science, signed_var)
    patches = lax.axis_size("patch")
    swaps = [(i, i + 1) for i in range(1, patches - 1, 2)]
    across = lax.ppermute(across, "patch", swaps + [(b, a) for a, b in swaps])
    inside = lax.ppermute(inside, "patch", [(i, i ^ 1) for i in range(patches)])

    def own_rows(*refs):
        own_kernel(shape, *refs)

    columns, weights, scale, science = pl.pallas_call(
        own_rows,
        out_shape=own_shapes,
        in_specs=vmem_specs(7),
        out_specs=vmem_specs(4),
        input_output_aliases={3: 0, 4: 1, 5: 2, 6: 3},
        compiler_params=grant(8),
        cost_estimate=estimate(1 << 28),
    )(arrived, science, signed_var, *own)

    def first(*refs):
        first_kernel(shape, *refs)

    def second(*refs):
        second_kernel(shape, *refs)

    normal = jax.ShapeDtypeStruct((STACK, LANE), jnp.float32)
    part, early_images, partial = pl.pallas_call(
        first,
        out_shape=(
            normal,
            jax.ShapeDtypeStruct((STEPS, rows - RAD, STACK, cols), jnp.float32),
            jax.ShapeDtypeStruct((STEPS, NPROF, RAD * SUB, cols), jnp.float32),
        ),
        in_specs=vmem_specs(5),
        out_specs=vmem_specs(3),
        compiler_params=grant(16),
        cost_estimate=estimate(1 << 28),
    )(inside, columns, weights, science, table)
    part, late_images = pl.pallas_call(
        second,
        out_shape=(normal, jax.ShapeDtypeStruct((STEPS, RAD, STACK, cols), jnp.float32)),
        in_specs=vmem_specs(6),
        out_specs=vmem_specs(2),
        compiler_params=grant(16),
        cost_estimate=estimate(1 << 28),
    )(across, weights, science, table, part, partial)

    parts, group = [part], 1
    while group < patches:
        if group > 1:
            parts = [sum(parts[1:], parts[0])]
        size = min(4, patches // group)
        for hop in range(group, size * group, group):
            pairs = [(i, i ^ hop) for i in range(patches)]
            parts.append(lax.ppermute(parts[0], "patch", pairs))
        group *= size

    def solve(*refs):
        solve_kernel(rows, cols, len(parts), *refs)

    return pl.pallas_call(
        solve,
        out_shape=held,
        in_specs=vmem_specs(len(parts) + 3),
        out_specs=pl.BlockSpec(memory_space=pl.ANY),
        scratch_shapes=[
            pltpu.VMEM(held.shape, held.dtype),
            pltpu.SemaphoreType.DMA((STEPS * PIECES,)),
        ],
        compiler_params=grant(16),
    )(*parts, scale, early_images, late_images)


def solution(mesh):
    return jax.shard_map(
        shards,
        mesh=mesh,
        in_specs=(
            P("visit", None, "patch", None),
            P(),
            P(None, "visit", "patch", None),
            P(None, "visit", "patch", None),
            P(None, "visit", "patch", None),
        ),
        out_specs=P(None, "visit", "patch", None),
        check_vma=False,
    )
```

time: 173 us -> 39.3 us (0.23)
  waiting for transfers between devices: 72.8 us -> 5.63 us
  other arithmetic: 24.9 us -> 1.92 us
  matrix products: 21.2 us -> 0 us
  between operations: 15.5 us -> 0.06 us
  local copies, waits for them, and re-layouts: 14.3 us -> 1.66 us
  Pallas kernels: 0 us -> 6.74 us
  blocking collectives: 14.6 us -> 10.6 us
  starting transfers between devices: 8.66 us -> 12.4 us
    psum x1 -> x0, waiting for transfers between devices: 72.1 us -> none  [from_root(): return lax.psum(block, axis)]
    dot_general x10 -> x0, matrix products: 18.8 us -> none  [the longest x2 4.8 us: shards(): jnp.einsum('cp,vp->vc', flattened, (weight * science[current]).reshape(vi...]
    another operation x12 -> x0, other arithmetic: 15.7 us -> none  [the longest x4 7.65 us: solve_kernel(): return jax.scipy.linalg.cho_solve((factor, True), normal_rhs)]
    psum x1 -> x0, blocking collectives: 14.6 us -> none  [shards(): summed_mat, summed_rhs = lax.psum((normal_mat, normal_rhs), 'patch')]
    all_to_all x0 -> x1, blocking collectives: none -> 10.6 us  [exchange(): lax.all_to_all(blocks, ('visit', 'patch'), 0, 0, axis_index_groups=groups...]
    unnamed x82 -> x2, local copies, waits for them, and re-layouts: 8.57 us -> 0.93 us
    all_to_all x0 -> x1, starting transfers between devices: none -> 7.25 us  [exchange(): lax.all_to_all(blocks, ('visit', 'patch'), 0, 0, axis_index_groups=groups...]
    pallas_call x0 -> x7, Pallas kernels: none -> 6.74 us  [the longest x1 1.92 us: shards(): pl.pallas_call(first, out_shape=(normal, jax.ShapeDtypeStruct((STEPS, row...]
  transfers between devices with their start and end apart: 5 -> 6, of which waited for: 2 -> 2; matrix products, arithmetic and copies ran while one was open for 3% -> 7% of each run, Pallas kernels for 0% -> 7%
where the time goes in v1:
time: 39.3 us; the launch traced here: 39 us
  starting transfers between devices  12.4 us (32%)
  blocking collectives  10.6 us (27%)
  Pallas kernels  6.74 us (17%)
  waiting for transfers between devices  5.63 us (14%)
  other arithmetic  1.92 us (5%)
  local copies, waits for them, and re-layouts  1.66 us (4%)
    all_to_all x1, blocking collectives, exchange(): lax.all_to_all(blocks, ('visit', 'patch'), 0, 0, axis_index_groups=groups...  10.6 us
    all_to_all x1, starting transfers between devices, exchange(): lax.all_to_all(blocks, ('visit', 'patch'), 0, 0, axis_index_groups=groups...  7.25 us
    ppermute x3, starting transfers between devices, shards(): parts.append(lax.ppermute(parts[0], 'patch', pairs))  4.38 us
    all_to_all x1, waiting for transfers between devices, exchange(): lax.all_to_all(blocks, ('visit', 'patch'), 0, 0, axis_index_groups=groups...  3.74 us
    pallas_call x1, Pallas kernels, shards(): pl.pallas_call(first, out_shape=(normal, jax.ShapeDtypeStruct((STEPS, row...  1.92 us
    pallas_call x1, Pallas kernels, shards(): pl.pallas_call(second, out_shape=(normal, jax.ShapeDtypeStruct((STEPS, RA...  1.9 us
    ppermute x3, waiting for transfers between devices, shards(): parts.append(lax.ppermute(parts[0], 'patch', pairs))  1.89 us
    pallas_call x1, Pallas kernels, shards(): pl.pallas_call(solve, out_shape=held, in_specs=vmem_specs(len(parts) + 3)...  1.87 us
  transfers between devices with their start and end apart: 6, of which 2 were waited for; matrix products, arithmetic and copies ran while one was open for 7% of the time, Pallas kernels for 7%

profile of v1, /device:TPU:0, one launch (start us, length us, event | category | flops | bytes accessed | tf_op | source)
XLA Modules:
  0.0 39.0 jit_solution(17005574146125194470)
XLA Ops:
  0.0 7.3 %all-to-all-start = ((f32[32,8,128]{2,1,0:T(8,128)}), f32[32,8,128]{2,1,0:T(8,128)S(1)}, u32[]{:S(2)}, u32[]{:S(2)}) async-start(f32[32,8,128]{2,1,0:T(8,128)} %bitcast.5), calls=%async_computation | async-start | bytes 262144 | tf_op jit(solution)/shard_map/all_to_all | solution.py:129
  7.3 1.0 %negate_select_fusion = (f32[2,1,16,1024]{3,2,1,0:T(8,128)S(1)}, pred[2,1,16,1024]{3,2,1,0:T(8,128)(4,1)S(1)}) fusion(f32[2,1,16,1024]{3,2,1,0:T(8,128)} %param.9, s32[2,1,16,1024]{3,2,1,0:T(8,128)} %param.10), kind=kLoop, calls=%fused_computation | loop fusion | flops 98304 | bytes 425984 | tf_op jit(solution)/shard_map/jit(_where)/select_n | solution.py:516
  8.3 0.7 %broadcast_in_dim.10.owners_in = s32[2,8,128]{2,1,0:T(8,128)S(1)} broadcast(s32[2]{0:T(128)} %param.7), dimensions={0} | broadcast | bytes 8200 | tf_op jit(solution)/shard_map/broadcast_in_dim | solution.py:518
  9.0 0.0 copy-start
  9.0 0.9 %copy-done = bf16[2,208,192]{2,1,0:T(8,128)(2,1)S(1)} copy-done((bf16[2,208,192]{2,1,0:T(8,128)(2,1)S(1)}, bf16[2,208,192]{2,1,0:T(8,128)(2,1)}, u32[]{:S(2)}) %copy-start) | copy-done | bytes 159768
  9.9 0.9 %broadcast_select_fusion.refs_1_ = f32[2,1,16,1024]{3,2,1,0:T(8,128)S(1)} fusion(pred[2,1,16,1024]{3,2,1,0:T(8,128)(4,1)S(1)} %get-tuple-element.40, f32[2,1,16,1024]{3,2,1,0:T(8,128)} %param.8), kind=kLoop, calls=%fused_computation.1 | loop fusion | flops 32768 | bytes 294912 | tf_op jit(solution)/shard_map/jit(_where)/select_n | solution.py:515
  10.9 3.7 %all-to-all-done.refs_3_ = f32[32,8,128]{2,1,0:T(8,128)S(1)} async-done(((f32[32,8,128]{2,1,0:T(8,128)}), f32[32,8,128]{2,1,0:T(8,128)S(1)}, u32[]{:S(2)}, u32[]{:S(2)}) %all-to-all-start) | async-done | bytes 131104 | tf_op jit(solution)/shard_map/all_to_all | solution.py:129
  14.6 10.6 %all_to_all.10.refs_0_ = f32[8,2,4,8,128]{4,3,2,1,0:T(8,128)S(1)} all-to-all(f32[8,2,4,8,128]{4,3,2,1,0:T(8,128)S(1)} %shard_map.65), channel_id=1, replica_groups={{0,4,8,12,16,20,24,28},{17,21,25,29,1,5,9,13},{2,6,10,14,18,22,26,30},{..., dimensions={0} | all-to-all | bytes 524288 | tf_op jit(solution)/shard_map/all_to_all | solution.py:129
  25.3 0.1 collective-permute-start.1
  25.4 0.7 %collective-permute-start = (f32[2,10,8,128]{3,2,1,0:T(8,128)S(1)}, f32[2,10,8,128]{3,2,1,0:T(8,128)S(1)}, u32[]{:S(2)}, u32[]{:S(2)}) collective-permute-start(f32[2,10,8,128]{3,2,1,0:T(8,128)S(1)} %get-tuple-element.24), channel_id=1, source_target_pairs={{1,2},{2,1},{5,6},{6,5},{9,10},{10,9},{13,14},{14,13},{17,18},{18,... | collective-permute-start | bytes 245768 | tf_op jit(solution)/shard_map/ppermute | solution.py:553
  26.1 1.0 %shard_map.67 = (bf16[2,5,3,16,1024]{4,3,2,1,0:T(8,128)(2,1)S(1)}, f32[2,16,1024]{2,1,0:T(8,128)S(1)}, f32[2,16,1024]{2,1,0:T(8,128)S(1)}, f32[2,16,1024]{2,1,0:T(8,128)S(1)}) custom-call(f32[8,2,4,8,128]{4,3,2,1,0:T(8,128)S(1)} %all_to_all.10.refs_0_, ...), custom_call_target="tpu_custom_call", output_to_operand_aliasing={{0}: (3, {}), {1}: (4, {}), {2}: (5, {}), {3}: (6, {})} | custom-call | flops 268435456 | bytes 1048576 | tf_op jit(solution)/shard_map/pallas_call | solution.py:559
  27.0 0.0 collective-permute-done.1.refs_0_
  27.0 1.9 %shard_map.68 = (f32[32,128]{1,0:T(8,128)S(1)}, f32[2,6,32,1024]{3,2,1,0:T(8,128)S(1)}, f32[2,5,80,1024]{3,2,1,0:T(8,128)S(1)}) custom-call(f32[2,10,8,128]{3,2,1,0:T(8,128)S(1)} %collective-permute-done.1.refs_0_, bf16[2,5,3,16,1024]{4,3,2,1,0:T(8,128)(2,1)S(1)} %get-tuple-element.32.refs_1_, f32[2,16,1024]{2,1,0:T(8,128)S(1)} %get-tuple-element.29.refs_2_.refs_1_, ...), custom_call_target="tpu_custom_call" | custom-call | flops 268435456 | bytes 1048576 | tf_op jit(solution)/shard_map/pallas_call | solution.py:576
  29.0 0.0 collective-permute-done.refs_0_
  29.0 1.9 %shard_map.69 = (f32[32,128]{1,0:T(8,128)S(1)}, f32[2,10,32,1024]{3,2,1,0:T(8,128)S(1)}) custom-call(f32[2,10,8,128]{3,2,1,0:T(8,128)S(1)} %collective-permute-done.refs_0_, f32[2,16,1024]{2,1,0:T(8,128)S(1)} %get-tuple-element.29.refs_2_.refs_1_, f32[2,16,1024]{2,1,0:T(8,128)S(1)} %get-tuple-element.30.refs_3_.refs_2_, ...), custom_call_target="tpu_custom_call" | custom-call | flops 268435456 | bytes 1048576 | tf_op jit(solution)/shard_map/pallas_call | solution.py:588
  30.9 1.0 %collective-permute-start.4 = (f32[32,128]{1,0:T(8,128)S(1)}, f32[32,128]{1,0:T(8,128)S(1)}, u32[]{:S(2)}, u32[]{:S(2)}) collective-permute-start(f32[32,128]{1,0:T(8,128)S(1)} %get-tuple-element.35.refs_0_), channel_id=1, source_target_pairs={{0,3},{1,2},{2,1},{3,0},{4,7},{5,6},{6,5},{7,4},{8,11},{9,10},{10,... | collective-permute-start | bytes 49160 | tf_op jit(solution)/shard_map/ppermute | solution.py:604
  31.9 3.4 %collective-permute-start.3 = (f32[32,128]{1,0:T(8,128)S(1)}, f32[32,128]{1,0:T(8,128)S(1)}, u32[]{:S(2)}, u32[]{:S(2)}) collective-permute-start(f32[32,128]{1,0:T(8,128)S(1)} %get-tuple-element.35.refs_0_), channel_id=1, source_target_pairs={{0,2},{1,3},{2,0},{3,1},{4,6},{5,7},{6,4},{7,5},{8,10},{9,11},{10,... | collective-permute-start | bytes 49160 | tf_op jit(solution)/shard_map/ppermute | solution.py:604
  35.2 0.0 collective-permute-start.2
  35.2 0.0 collective-permute-done.4.refs_3_
  35.3 1.9 %collective-permute-done.3.refs_2_ = f32[32,128]{1,0:T(8,128)S(1)} collective-permute-done((f32[32,128]{1,0:T(8,128)S(1)}, f32[32,128]{1,0:T(8,128)S(1)}, u32[]{:S(2)}, u32[]{:S(2)}) %collective-permute-start.3) | collective-permute-done | bytes 16416 | tf_op jit(solution)/shard_map/ppermute | solution.py:604
  37.1 0.0 collective-permute-done.2.refs_1_
  37.1 1.9 %shard_map.70 = f32[2,1,16,1024]{3,2,1,0:T(8,128)} custom-call(f32[32,128]{1,0:T(8,128)S(1)} %get-tuple-element.35.refs_0_, f32[32,128]{1,0:T(8,128)S(1)} %collective-permute-done.2.refs_1_, f32[32,128]{1,0:T(8,128)S(1)} %collective-permute-done.3.refs_2_, f32[32,128]{1,0:T(8,128)S(1)} %collective-permute-done.4.refs_3_, ...), custom_call_target="tpu_custom_call" | custom-call | tf_op jit(solution)/shard_map/pallas_call | solution.py:610
  (3 shorter events, 0.1 us)
Async XLA Ops:
  0.0 14.6 %all-to-all-start = ((f32[32,8,128]{2,1,0:T(8,128)}), f32[32,8,128]{2,1,0:T(8,128)S(1)}, u32[]{:S(2)}, u32[]{:S(2)}) async-start(f32[32,8,128]{2,1,0:T(8,128)} %bitcast.5), calls=%async_computation | async-start | bytes 262144 | tf_op jit(solution)/shard_map/all_to_all | solution.py:129
  9.0 0.9 %copy-start = (bf16[2,208,192]{2,1,0:T(8,128)(2,1)S(1)}, bf16[2,208,192]{2,1,0:T(8,128)(2,1)}, u32[]{:S(2)}) copy-start(bf16[2,208,192]{2,1,0:T(8,128)(2,1)} %constant.6.clone.table_in) | copy-start | bytes 479236
  25.3 1.7 %collective-permute-start.1 = (f32[2,10,8,128]{3,2,1,0:T(8,128)S(1)}, f32[2,10,8,128]{3,2,1,0:T(8,128)S(1)}, u32[]{:S(2)}, u32[]{:S(2)}) collective-permute-start(f32[2,10,8,128]{3,2,1,0:T(8,128)S(1)} %get-tuple-element.31), channel_id=1, source_target_pairs={{0,1},{1,0},{2,3},{3,2},{4,5},{5,4},{6,7},{7,6},{8,9},{9,8},{10,11... | collective-permute-start | bytes 245768 | tf_op jit(solution)/shard_map/ppermute | solution.py:554
  25.4 3.6 %collective-permute-start = (f32[2,10,8,128]{3,2,1,0:T(8,128)S(1)}, f32[2,10,8,128]{3,2,1,0:T(8,128)S(1)}, u32[]{:S(2)}, u32[]{:S(2)}) collective-permute-start(f32[2,10,8,128]{3,2,1,0:T(8,128)S(1)} %get-tuple-element.24), channel_id=1, source_target_pairs={{1,2},{2,1},{5,6},{6,5},{9,10},{10,9},{13,14},{14,13},{17,18},{18,... | collective-permute-start | bytes 245768 | tf_op jit(solution)/shard_map/ppermute | solution.py:553
  30.9 4.4 %collective-permute-start.4 = (f32[32,128]{1,0:T(8,128)S(1)}, f32[32,128]{1,0:T(8,128)S(1)}, u32[]{:S(2)}, u32[]{:S(2)}) collective-permute-start(f32[32,128]{1,0:T(8,128)S(1)} %get-tuple-element.35.refs_0_), channel_id=1, source_target_pairs={{0,3},{1,2},{2,1},{3,0},{4,7},{5,6},{6,5},{7,4},{8,11},{9,10},{10,... | collective-permute-start | bytes 49160 | tf_op jit(solution)/shard_map/ppermute | solution.py:604
  31.9 5.2 %collective-permute-start.3 = (f32[32,128]{1,0:T(8,128)S(1)}, f32[32,128]{1,0:T(8,128)S(1)}, u32[]{:S(2)}, u32[]{:S(2)}) collective-permute-start(f32[32,128]{1,0:T(8,128)S(1)} %get-tuple-element.35.refs_0_), channel_id=1, source_target_pairs={{0,2},{1,3},{2,0},{3,1},{4,6},{5,7},{6,4},{7,5},{8,10},{9,11},{10,... | collective-permute-start | bytes 49160 | tf_op jit(solution)/shard_map/ppermute | solution.py:604
  35.2 1.9 %collective-permute-start.2 = (f32[32,128]{1,0:T(8,128)S(1)}, f32[32,128]{1,0:T(8,128)S(1)}, u32[]{:S(2)}, u32[]{:S(2)}) collective-permute-start(f32[32,128]{1,0:T(8,128)S(1)} %get-tuple-element.35.refs_0_), channel_id=1, source_target_pairs={{0,1},{1,0},{2,3},{3,2},{4,5},{5,4},{6,7},{7,6},{8,9},{9,8},{10,11... | collective-permute-start | bytes 49160 | tf_op jit(solution)/shard_map/ppermute | solution.py:604

commit v2 on v1

--- a/solution.py
+++ b/solution.py
@@ -109,7 +109,7 @@
 
 
 def pick_kernel(visits, per, owners, science, table, got, out):
-    turn = (visits // 2) * patch_parity()
+    turn = visits - visits // 2 - 1 + patch_parity()
     for s in range(STEPS):
         place = lax.rem(owners[s] + turn, jnp.full((SUB, LANE), visits))
         for n in range(per):
@@ -123,7 +123,7 @@
 def exchange(blocks):
     visits, patches = lax.axis_size("visit"), lax.axis_size("patch")
     groups = [
-        [(n + (visits // 2) * (p % 2)) % visits * patches + p for n in range(visits)]
+        [(n + visits // 2 + 1 - p % 2) % visits * patches + p for n in range(visits)]
         for p in range(patches)
     ]
     return lax.all_to_all(

time: 39.3 us -> 36.4 us (0.926)
  waiting for transfers between devices: 5.63 us -> 2.47 us
  starting transfers between devices: 12.4 us -> 13.4 us
  blocking collectives: 10.6 us -> 9.89 us
    all_to_all x1, waiting for transfers between devices: 3.74 us -> 0.58 us  [exchange(): lax.all_to_all(blocks, ('visit', 'patch'), 0, 0, axis_index_groups=groups...]
    all_to_all x1, starting transfers between devices: 7.25 us -> 8.25 us  [exchange(): lax.all_to_all(blocks, ('visit', 'patch'), 0, 0, axis_index_groups=groups...]
    all_to_all x1, blocking collectives: 10.6 us -> 9.89 us  [exchange(): lax.all_to_all(blocks, ('visit', 'patch'), 0, 0, axis_index_groups=groups...]
  transfers between devices with their start and end apart: 6 -> 6, of which waited for: 2 -> 2; matrix products, arithmetic and copies ran while one was open for 7% -> 7% of each run, Pallas kernels for 7% -> 8%
where the time goes in v2:
time: 36.4 us; the launch traced here: 36.1 us
  starting transfers between devices  13.4 us (37%)
  blocking collectives  9.89 us (27%)
  Pallas kernels  6.74 us (19%)
  waiting for transfers between devices  2.47 us (7%)
  other arithmetic  1.92 us (5%)
  local copies, waits for them, and re-layouts  1.66 us (5%)
    all_to_all x1, blocking collectives, exchange(): lax.all_to_all(blocks, ('visit', 'patch'), 0, 0, axis_index_groups=groups...  9.89 us
    all_to_all x1, starting transfers between devices, exchange(): lax.all_to_all(blocks, ('visit', 'patch'), 0, 0, axis_index_groups=groups...  8.25 us
    ppermute x3, starting transfers between devices, shards(): parts.append(lax.ppermute(parts[0], 'patch', pairs))  4.38 us
    pallas_call x1, Pallas kernels, shards(): pl.pallas_call(first, out_shape=(normal, jax.ShapeDtypeStruct((STEPS, row...  1.92 us
    pallas_call x1, Pallas kernels, shards(): pl.pallas_call(second, out_shape=(normal, jax.ShapeDtypeStruct((STEPS, RA...  1.9 us
    ppermute x3, waiting for transfers between devices, shards(): parts.append(lax.ppermute(parts[0], 'patch', pairs))  1.89 us
    pallas_call x1, Pallas kernels, shards(): pl.pallas_call(solve, out_shape=held, in_specs=vmem_specs(len(parts) + 3)...  1.87 us
    select_n x1, other arithmetic, shards(): signed_var = jnp.where(bad, -sci_var, sci_var)  1 us
  transfers between devices with their start and end apart: 6, of which 2 were waited for; matrix products, arithmetic and copies ran while one was open for 7% of the time, Pallas kernels for 8%

profile of v2, /device:TPU:0, one launch (start us, length us, event | category | flops | bytes accessed | tf_op | source)
XLA Modules:
  0.0 36.1 jit_solution(18161422612482083934)
XLA Ops:
  0.0 8.2 %all-to-all-start = ((f32[32,8,128]{2,1,0:T(8,128)}), f32[32,8,128]{2,1,0:T(8,128)S(1)}, u32[]{:S(2)}, u32[]{:S(2)}) async-start(f32[32,8,128]{2,1,0:T(8,128)} %bitcast.5), calls=%async_computation | async-start | bytes 262144 | tf_op jit(solution)/shard_map/all_to_all | solution.py:129
  8.2 1.0 %negate_select_fusion = (f32[2,1,16,1024]{3,2,1,0:T(8,128)S(1)}, pred[2,1,16,1024]{3,2,1,0:T(8,128)(4,1)S(1)}) fusion(f32[2,1,16,1024]{3,2,1,0:T(8,128)} %param.9, s32[2,1,16,1024]{3,2,1,0:T(8,128)} %param.10), kind=kLoop, calls=%fused_computation | loop fusion | flops 98304 | bytes 425984 | tf_op jit(solution)/shard_map/jit(_where)/select_n | solution.py:516
  9.2 0.7 %broadcast_in_dim.10.owners_in = s32[2,8,128]{2,1,0:T(8,128)S(1)} broadcast(s32[2]{0:T(128)} %param.7), dimensions={0} | broadcast | bytes 8200 | tf_op jit(solution)/shard_map/broadcast_in_dim | solution.py:518
  10.0 0.0 copy-start
  10.0 0.9 %copy-done = bf16[2,208,192]{2,1,0:T(8,128)(2,1)S(1)} copy-done((bf16[2,208,192]{2,1,0:T(8,128)(2,1)S(1)}, bf16[2,208,192]{2,1,0:T(8,128)(2,1)}, u32[]{:S(2)}) %copy-start) | copy-done | bytes 159768
  10.9 0.9 %broadcast_select_fusion.refs_1_ = f32[2,1,16,1024]{3,2,1,0:T(8,128)S(1)} fusion(pred[2,1,16,1024]{3,2,1,0:T(8,128)(4,1)S(1)} %get-tuple-element.40, f32[2,1,16,1024]{3,2,1,0:T(8,128)} %param.8), kind=kLoop, calls=%fused_computation.1 | loop fusion | flops 32768 | bytes 294912 | tf_op jit(solution)/shard_map/jit(_where)/select_n | solution.py:515
  11.9 0.6 %all-to-all-done.refs_3_ = f32[32,8,128]{2,1,0:T(8,128)S(1)} async-done(((f32[32,8,128]{2,1,0:T(8,128)}), f32[32,8,128]{2,1,0:T(8,128)S(1)}, u32[]{:S(2)}, u32[]{:S(2)}) %all-to-all-start) | async-done | bytes 131104 | tf_op jit(solution)/shard_map/all_to_all | solution.py:129
  12.5 9.9 %all_to_all.10.refs_0_ = f32[8,2,4,8,128]{4,3,2,1,0:T(8,128)S(1)} all-to-all(f32[8,2,4,8,128]{4,3,2,1,0:T(8,128)S(1)} %shard_map.65), channel_id=1, replica_groups={{20,24,28,0,4,8,12,16},{17,21,25,29,1,5,9,13},{22,26,30,2,6,10,14,18},{..., dimensions={0} | all-to-all | bytes 524288 | tf_op jit(solution)/shard_map/all_to_all | solution.py:129
  22.4 0.1 collective-permute-start.1
  22.5 0.7 %collective-permute-start = (f32[2,10,8,128]{3,2,1,0:T(8,128)S(1)}, f32[2,10,8,128]{3,2,1,0:T(8,128)S(1)}, u32[]{:S(2)}, u32[]{:S(2)}) collective-permute-start(f32[2,10,8,128]{3,2,1,0:T(8,128)S(1)} %get-tuple-element.24), channel_id=1, source_target_pairs={{1,2},{2,1},{5,6},{6,5},{9,10},{10,9},{13,14},{14,13},{17,18},{18,... | collective-permute-start | bytes 245768 | tf_op jit(solution)/shard_map/ppermute | solution.py:553
  23.1 1.0 %shard_map.67 = (bf16[2,5,3,16,1024]{4,3,2,1,0:T(8,128)(2,1)S(1)}, f32[2,16,1024]{2,1,0:T(8,128)S(1)}, f32[2,16,1024]{2,1,0:T(8,128)S(1)}, f32[2,16,1024]{2,1,0:T(8,128)S(1)}) custom-call(f32[8,2,4,8,128]{4,3,2,1,0:T(8,128)S(1)} %all_to_all.10.refs_0_, ...), custom_call_target="tpu_custom_call", output_to_operand_aliasing={{0}: (3, {}), {1}: (4, {}), {2}: (5, {}), {3}: (6, {})} | custom-call | flops 268435456 | bytes 1048576 | tf_op jit(solution)/shard_map/pallas_call | solution.py:559
  24.1 0.0 collective-permute-done.1.refs_0_
  24.1 1.9 %shard_map.68 = (f32[32,128]{1,0:T(8,128)S(1)}, f32[2,6,32,1024]{3,2,1,0:T(8,128)S(1)}, f32[2,5,80,1024]{3,2,1,0:T(8,128)S(1)}) custom-call(f32[2,10,8,128]{3,2,1,0:T(8,128)S(1)} %collective-permute-done.1.refs_0_, bf16[2,5,3,16,1024]{4,3,2,1,0:T(8,128)(2,1)S(1)} %get-tuple-element.32.refs_1_, f32[2,16,1024]{2,1,0:T(8,128)S(1)} %get-tuple-element.29.refs_2_.refs_1_, ...), custom_call_target="tpu_custom_call" | custom-call | flops 268435456 | bytes 1048576 | tf_op jit(solution)/shard_map/pallas_call | solution.py:576
  26.1 0.0 collective-permute-done.refs_0_
  26.1 1.9 %shard_map.69 = (f32[32,128]{1,0:T(8,128)S(1)}, f32[2,10,32,1024]{3,2,1,0:T(8,128)S(1)}) custom-call(f32[2,10,8,128]{3,2,1,0:T(8,128)S(1)} %collective-permute-done.refs_0_, f32[2,16,1024]{2,1,0:T(8,128)S(1)} %get-tuple-element.29.refs_2_.refs_1_, f32[2,16,1024]{2,1,0:T(8,128)S(1)} %get-tuple-element.30.refs_3_.refs_2_, ...), custom_call_target="tpu_custom_call" | custom-call | flops 268435456 | bytes 1048576 | tf_op jit(solution)/shard_map/pallas_call | solution.py:588
  28.0 1.0 %collective-permute-start.4 = (f32[32,128]{1,0:T(8,128)S(1)}, f32[32,128]{1,0:T(8,128)S(1)}, u32[]{:S(2)}, u32[]{:S(2)}) collective-permute-start(f32[32,128]{1,0:T(8,128)S(1)} %get-tuple-element.35.refs_0_), channel_id=1, source_target_pairs={{0,3},{1,2},{2,1},{3,0},{4,7},{5,6},{6,5},{7,4},{8,11},{9,10},{10,... | collective-permute-start | bytes 49160 | tf_op jit(solution)/shard_map/ppermute | solution.py:604
  29.0 3.4 %collective-permute-start.3 = (f32[32,128]{1,0:T(8,128)S(1)}, f32[32,128]{1,0:T(8,128)S(1)}, u32[]{:S(2)}, u32[]{:S(2)}) collective-permute-start(f32[32,128]{1,0:T(8,128)S(1)} %get-tuple-element.35.refs_0_), channel_id=1, source_target_pairs={{0,2},{1,3},{2,0},{3,1},{4,6},{5,7},{6,4},{7,5},{8,10},{9,11},{10,... | collective-permute-start | bytes 49160 | tf_op jit(solution)/shard_map/ppermute | solution.py:604
  32.3 0.0 collective-permute-start.2
  32.3 0.0 collective-permute-done.4.refs_3_
  32.3 1.9 %collective-permute-done.3.refs_2_ = f32[32,128]{1,0:T(8,128)S(1)} collective-permute-done((f32[32,128]{1,0:T(8,128)S(1)}, f32[32,128]{1,0:T(8,128)S(1)}, u32[]{:S(2)}, u32[]{:S(2)}) %collective-permute-start.3) | collective-permute-done | bytes 16416 | tf_op jit(solution)/shard_map/ppermute | solution.py:604
  34.2 0.0 collective-permute-done.2.refs_1_
  34.2 1.9 %shard_map.70 = f32[2,1,16,1024]{3,2,1,0:T(8,128)} custom-call(f32[32,128]{1,0:T(8,128)S(1)} %get-tuple-element.35.refs_0_, f32[32,128]{1,0:T(8,128)S(1)} %collective-permute-done.2.refs_1_, f32[32,128]{1,0:T(8,128)S(1)} %collective-permute-done.3.refs_2_, f32[32,128]{1,0:T(8,128)S(1)} %collective-permute-done.4.refs_3_, ...), custom_call_target="tpu_custom_call" | custom-call | tf_op jit(solution)/shard_map/pallas_call | solution.py:610
  (3 shorter events, 0.1 us)
Async XLA Ops:
  0.0 12.4 %all-to-all-start = ((f32[32,8,128]{2,1,0:T(8,128)}), f32[32,8,128]{2,1,0:T(8,128)S(1)}, u32[]{:S(2)}, u32[]{:S(2)}) async-start(f32[32,8,128]{2,1,0:T(8,128)} %bitcast.5), calls=%async_computation | async-start | bytes 262144 | tf_op jit(solution)/shard_map/all_to_all | solution.py:129
  10.0 0.9 %copy-start = (bf16[2,208,192]{2,1,0:T(8,128)(2,1)S(1)}, bf16[2,208,192]{2,1,0:T(8,128)(2,1)}, u32[]{:S(2)}) copy-start(bf16[2,208,192]{2,1,0:T(8,128)(2,1)} %constant.6.clone.table_in) | copy-start | bytes 479236
  22.4 1.7 %collective-permute-start.1 = (f32[2,10,8,128]{3,2,1,0:T(8,128)S(1)}, f32[2,10,8,128]{3,2,1,0:T(8,128)S(1)}, u32[]{:S(2)}, u32[]{:S(2)}) collective-permute-start(f32[2,10,8,128]{3,2,1,0:T(8,128)S(1)} %get-tuple-element.31), channel_id=1, source_target_pairs={{0,1},{1,0},{2,3},{3,2},{4,5},{5,4},{6,7},{7,6},{8,9},{9,8},{10,11... | collective-permute-start | bytes 245768 | tf_op jit(solution)/shard_map/ppermute | solution.py:554
  22.5 3.6 %collective-permute-start = (f32[2,10,8,128]{3,2,1,0:T(8,128)S(1)}, f32[2,10,8,128]{3,2,1,0:T(8,128)S(1)}, u32[]{:S(2)}, u32[]{:S(2)}) collective-permute-start(f32[2,10,8,128]{3,2,1,0:T(8,128)S(1)} %get-tuple-element.24), channel_id=1, source_target_pairs={{1,2},{2,1},{5,6},{6,5},{9,10},{10,9},{13,14},{14,13},{17,18},{18,... | collective-permute-start | bytes 245768 | tf_op jit(solution)/shard_map/ppermute | solution.py:553
  28.0 4.4 %collective-permute-start.4 = (f32[32,128]{1,0:T(8,128)S(1)}, f32[32,128]{1,0:T(8,128)S(1)}, u32[]{:S(2)}, u32[]{:S(2)}) collective-permute-start(f32[32,128]{1,0:T(8,128)S(1)} %get-tuple-element.35.refs_0_), channel_id=1, source_target_pairs={{0,3},{1,2},{2,1},{3,0},{4,7},{5,6},{6,5},{7,4},{8,11},{9,10},{10,... | collective-permute-start | bytes 49160 | tf_op jit(solution)/shard_map/ppermute | solution.py:604
  29.0 5.2 %collective-permute-start.3 = (f32[32,128]{1,0:T(8,128)S(1)}, f32[32,128]{1,0:T(8,128)S(1)}, u32[]{:S(2)}, u32[]{:S(2)}) collective-permute-start(f32[32,128]{1,0:T(8,128)S(1)} %get-tuple-element.35.refs_0_), channel_id=1, source_target_pairs={{0,2},{1,3},{2,0},{3,1},{4,6},{5,7},{6,4},{7,5},{8,10},{9,11},{10,... | collective-permute-start | bytes 49160 | tf_op jit(solution)/shard_map/ppermute | solution.py:604
  32.3 1.9 %collective-permute-start.2 = (f32[32,128]{1,0:T(8,128)S(1)}, f32[32,128]{1,0:T(8,128)S(1)}, u32[]{:S(2)}, u32[]{:S(2)}) collective-permute-start(f32[32,128]{1,0:T(8,128)S(1)} %get-tuple-element.35.refs_0_), channel_id=1, source_target_pairs={{0,1},{1,0},{2,3},{3,2},{4,5},{5,4},{6,7},{7,6},{8,9},{9,8},{10,11... | collective-permute-start | bytes 49160 | tf_op jit(solution)/shard_map/ppermute | solution.py:604

commit v3 on v2

--- a/solution.py
+++ b/solution.py
@@ -109,7 +109,7 @@
 
 
 def pick_kernel(visits, per, owners, science, table, got, out):
-    turn = visits - visits // 2 - 1 + patch_parity()
+    turn = visits - visits // 2 - 2 * (1 - patch_parity())
     for s in range(STEPS):
         place = lax.rem(owners[s] + turn, jnp.full((SUB, LANE), visits))
         for n in range(per):
@@ -123,7 +123,7 @@
 def exchange(blocks):
     visits, patches = lax.axis_size("visit"), lax.axis_size("patch")
     groups = [
-        [(n + visits // 2 + 1 - p % 2) % visits * patches + p for n in range(visits)]
+        [(n + visits // 2 + 2 * (1 - p % 2)) % visits * patches + p for n in range(visits)]
         for p in range(patches)
     ]
     return lax.all_to_all(

time: 36.4 us -> 37 us (1.016)
  blocking collectives: 9.89 us -> 10.4 us
    all_to_all x1, blocking collectives: 9.89 us -> 10.4 us  [exchange(): lax.all_to_all(blocks, ('visit', 'patch'), 0, 0, axis_index_groups=groups...]
where the time goes in v3:
time: 37 us; the launch traced here: 36.6 us
  starting transfers between devices  13.4 us (36%)
  blocking collectives  10.4 us (28%)
  Pallas kernels  6.74 us (18%)
  waiting for transfers between devices  2.39 us (6%)
  other arithmetic  1.92 us (5%)
  local copies, waits for them, and re-layouts  1.66 us (4%)
    all_to_all x1, blocking collectives, exchange(): lax.all_to_all(blocks, ('visit', 'patch'), 0, 0, axis_index_groups=groups...  10.4 us
    all_to_all x1, starting transfers between devices, exchange(): lax.all_to_all(blocks, ('visit', 'patch'), 0, 0, axis_index_groups=groups...  8.33 us
    ppermute x3, starting transfers between devices, shards(): parts.append(lax.ppermute(parts[0], 'patch', pairs))  4.37 us
    pallas_call x1, Pallas kernels, shards(): pl.pallas_call(first, out_shape=(normal, jax.ShapeDtypeStruct((STEPS, row...  1.92 us
    pallas_call x1, Pallas kernels, shards(): pl.pallas_call(second, out_shape=(normal, jax.ShapeDtypeStruct((STEPS, RA...  1.9 us
    ppermute x3, waiting for transfers between devices, shards(): parts.append(lax.ppermute(parts[0], 'patch', pairs))  1.89 us
    pallas_call x1, Pallas kernels, shards(): pl.pallas_call(solve, out_shape=held, in_specs=vmem_specs(len(parts) + 3)...  1.87 us
    select_n x1, other arithmetic, shards(): signed_var = jnp.where(bad, -sci_var, sci_var)  1 us
  transfers between devices with their start and end apart: 6, of which 2 were waited for; matrix products, arithmetic and copies ran while one was open for 7% of the time, Pallas kernels for 8%

profile of v3, /device:TPU:0, one launch (start us, length us, event | category | flops | bytes accessed | tf_op | source)
XLA Modules:
  0.0 36.6 jit_solution(9065863327438034644)
XLA Ops:
  0.0 8.3 %all-to-all-start = ((f32[32,8,128]{2,1,0:T(8,128)}), f32[32,8,128]{2,1,0:T(8,128)S(1)}, u32[]{:S(2)}, u32[]{:S(2)}) async-start(f32[32,8,128]{2,1,0:T(8,128)} %bitcast.5), calls=%async_computation | async-start | bytes 262144 | tf_op jit(solution)/shard_map/all_to_all | solution.py:129
  8.3 1.0 %negate_select_fusion = (f32[2,1,16,1024]{3,2,1,0:T(8,128)S(1)}, pred[2,1,16,1024]{3,2,1,0:T(8,128)(4,1)S(1)}) fusion(f32[2,1,16,1024]{3,2,1,0:T(8,128)} %param.9, s32[2,1,16,1024]{3,2,1,0:T(8,128)} %param.10), kind=kLoop, calls=%fused_computation | loop fusion | flops 98304 | bytes 425984 | tf_op jit(solution)/shard_map/jit(_where)/select_n | solution.py:516
  9.3 0.7 %broadcast_in_dim.10.owners_in = s32[2,8,128]{2,1,0:T(8,128)S(1)} broadcast(s32[2]{0:T(128)} %param.7), dimensions={0} | broadcast | bytes 8200 | tf_op jit(solution)/shard_map/broadcast_in_dim | solution.py:518
  10.1 0.0 copy-start
  10.1 0.9 %copy-done = bf16[2,208,192]{2,1,0:T(8,128)(2,1)S(1)} copy-done((bf16[2,208,192]{2,1,0:T(8,128)(2,1)S(1)}, bf16[2,208,192]{2,1,0:T(8,128)(2,1)}, u32[]{:S(2)}) %copy-start) | copy-done | bytes 159768
  11.0 0.9 %broadcast_select_fusion.refs_1_ = f32[2,1,16,1024]{3,2,1,0:T(8,128)S(1)} fusion(pred[2,1,16,1024]{3,2,1,0:T(8,128)(4,1)S(1)} %get-tuple-element.40, f32[2,1,16,1024]{3,2,1,0:T(8,128)} %param.8), kind=kLoop, calls=%fused_computation.1 | loop fusion | flops 32768 | bytes 294912 | tf_op jit(solution)/shard_map/jit(_where)/select_n | solution.py:515
  11.9 0.5 %all-to-all-done.refs_3_ = f32[32,8,128]{2,1,0:T(8,128)S(1)} async-done(((f32[32,8,128]{2,1,0:T(8,128)}), f32[32,8,128]{2,1,0:T(8,128)S(1)}, u32[]{:S(2)}, u32[]{:S(2)}) %all-to-all-start) | async-done | bytes 131104 | tf_op jit(solution)/shard_map/all_to_all | solution.py:129
  12.5 10.4 %all_to_all.10.refs_0_ = f32[8,2,4,8,128]{4,3,2,1,0:T(8,128)S(1)} all-to-all(f32[8,2,4,8,128]{4,3,2,1,0:T(8,128)S(1)} %shard_map.65), channel_id=1, replica_groups={{24,28,0,4,8,12,16,20},{17,21,25,29,1,5,9,13},{26,30,2,6,10,14,18,22},{..., dimensions={0} | all-to-all | bytes 524288 | tf_op jit(solution)/shard_map/all_to_all | solution.py:129
  22.9 0.1 collective-permute-start.1
  23.0 0.7 %collective-permute-start = (f32[2,10,8,128]{3,2,1,0:T(8,128)S(1)}, f32[2,10,8,128]{3,2,1,0:T(8,128)S(1)}, u32[]{:S(2)}, u32[]{:S(2)}) collective-permute-start(f32[2,10,8,128]{3,2,1,0:T(8,128)S(1)} %get-tuple-element.24), channel_id=1, source_target_pairs={{1,2},{2,1},{5,6},{6,5},{9,10},{10,9},{13,14},{14,13},{17,18},{18,... | collective-permute-start | bytes 245768 | tf_op jit(solution)/shard_map/ppermute | solution.py:553
  23.7 1.0 %shard_map.67 = (bf16[2,5,3,16,1024]{4,3,2,1,0:T(8,128)(2,1)S(1)}, f32[2,16,1024]{2,1,0:T(8,128)S(1)}, f32[2,16,1024]{2,1,0:T(8,128)S(1)}, f32[2,16,1024]{2,1,0:T(8,128)S(1)}) custom-call(f32[8,2,4,8,128]{4,3,2,1,0:T(8,128)S(1)} %all_to_all.10.refs_0_, ...), custom_call_target="tpu_custom_call", output_to_operand_aliasing={{0}: (3, {}), {1}: (4, {}), {2}: (5, {}), {3}: (6, {})} | custom-call | flops 268435456 | bytes 1048576 | tf_op jit(solution)/shard_map/pallas_call | solution.py:559
  24.7 0.0 collective-permute-done.1.refs_0_
  24.7 1.9 %shard_map.68 = (f32[32,128]{1,0:T(8,128)S(1)}, f32[2,6,32,1024]{3,2,1,0:T(8,128)S(1)}, f32[2,5,80,1024]{3,2,1,0:T(8,128)S(1)}) custom-call(f32[2,10,8,128]{3,2,1,0:T(8,128)S(1)} %collective-permute-done.1.refs_0_, bf16[2,5,3,16,1024]{4,3,2,1,0:T(8,128)(2,1)S(1)} %get-tuple-element.32.refs_1_, f32[2,16,1024]{2,1,0:T(8,128)S(1)} %get-tuple-element.29.refs_2_.refs_1_, ...), custom_call_target="tpu_custom_call" | custom-call | flops 268435456 | bytes 1048576 | tf_op jit(solution)/shard_map/pallas_call | solution.py:576
  26.6 0.0 collective-permute-done.refs_0_
  26.6 1.9 %shard_map.69 = (f32[32,128]{1,0:T(8,128)S(1)}, f32[2,10,32,1024]{3,2,1,0:T(8,128)S(1)}) custom-call(f32[2,10,8,128]{3,2,1,0:T(8,128)S(1)} %collective-permute-done.refs_0_, f32[2,16,1024]{2,1,0:T(8,128)S(1)} %get-tuple-element.29.refs_2_.refs_1_, f32[2,16,1024]{2,1,0:T(8,128)S(1)} %get-tuple-element.30.refs_3_.refs_2_, ...), custom_call_target="tpu_custom_call" | custom-call | flops 268435456 | bytes 1048576 | tf_op jit(solution)/shard_map/pallas_call | solution.py:588
  28.5 1.0 %collective-permute-start.4 = (f32[32,128]{1,0:T(8,128)S(1)}, f32[32,128]{1,0:T(8,128)S(1)}, u32[]{:S(2)}, u32[]{:S(2)}) collective-permute-start(f32[32,128]{1,0:T(8,128)S(1)} %get-tuple-element.35.refs_0_), channel_id=1, source_target_pairs={{0,3},{1,2},{2,1},{3,0},{4,7},{5,6},{6,5},{7,4},{8,11},{9,10},{10,... | collective-permute-start | bytes 49160 | tf_op jit(solution)/shard_map/ppermute | solution.py:604
  29.5 3.4 %collective-permute-start.3 = (f32[32,128]{1,0:T(8,128)S(1)}, f32[32,128]{1,0:T(8,128)S(1)}, u32[]{:S(2)}, u32[]{:S(2)}) collective-permute-start(f32[32,128]{1,0:T(8,128)S(1)} %get-tuple-element.35.refs_0_), channel_id=1, source_target_pairs={{0,2},{1,3},{2,0},{3,1},{4,6},{5,7},{6,4},{7,5},{8,10},{9,11},{10,... | collective-permute-start | bytes 49160 | tf_op jit(solution)/shard_map/ppermute | solution.py:604
  32.9 0.0 collective-permute-start.2
  32.9 0.0 collective-permute-done.4.refs_3_
  32.9 1.9 %collective-permute-done.3.refs_2_ = f32[32,128]{1,0:T(8,128)S(1)} collective-permute-done((f32[32,128]{1,0:T(8,128)S(1)}, f32[32,128]{1,0:T(8,128)S(1)}, u32[]{:S(2)}, u32[]{:S(2)}) %collective-permute-start.3) | collective-permute-done | bytes 16416 | tf_op jit(solution)/shard_map/ppermute | solution.py:604
  34.8 0.0 collective-permute-done.2.refs_1_
  34.8 1.9 %shard_map.70 = f32[2,1,16,1024]{3,2,1,0:T(8,128)} custom-call(f32[32,128]{1,0:T(8,128)S(1)} %get-tuple-element.35.refs_0_, f32[32,128]{1,0:T(8,128)S(1)} %collective-permute-done.2.refs_1_, f32[32,128]{1,0:T(8,128)S(1)} %collective-permute-done.3.refs_2_, f32[32,128]{1,0:T(8,128)S(1)} %collective-permute-done.4.refs_3_, ...), custom_call_target="tpu_custom_call" | custom-call | tf_op jit(solution)/shard_map/pallas_call | solution.py:610
  (3 shorter events, 0.1 us)
Async XLA Ops:
  0.0 12.4 %all-to-all-start = ((f32[32,8,128]{2,1,0:T(8,128)}), f32[32,8,128]{2,1,0:T(8,128)S(1)}, u32[]{:S(2)}, u32[]{:S(2)}) async-start(f32[32,8,128]{2,1,0:T(8,128)} %bitcast.5), calls=%async_computation | async-start | bytes 262144 | tf_op jit(solution)/shard_map/all_to_all | solution.py:129
  10.1 0.9 %copy-start = (bf16[2,208,192]{2,1,0:T(8,128)(2,1)S(1)}, bf16[2,208,192]{2,1,0:T(8,128)(2,1)}, u32[]{:S(2)}) copy-start(bf16[2,208,192]{2,1,0:T(8,128)(2,1)} %constant.6.clone.table_in) | copy-start | bytes 479236
  22.9 1.7 %collective-permute-start.1 = (f32[2,10,8,128]{3,2,1,0:T(8,128)S(1)}, f32[2,10,8,128]{3,2,1,0:T(8,128)S(1)}, u32[]{:S(2)}, u32[]{:S(2)}) collective-permute-start(f32[2,10,8,128]{3,2,1,0:T(8,128)S(1)} %get-tuple-element.31), channel_id=1, source_target_pairs={{0,1},{1,0},{2,3},{3,2},{4,5},{5,4},{6,7},{7,6},{8,9},{9,8},{10,11... | collective-permute-start | bytes 245768 | tf_op jit(solution)/shard_map/ppermute | solution.py:554
  23.0 3.6 %collective-permute-start = (f32[2,10,8,128]{3,2,1,0:T(8,128)S(1)}, f32[2,10,8,128]{3,2,1,0:T(8,128)S(1)}, u32[]{:S(2)}, u32[]{:S(2)}) collective-permute-start(f32[2,10,8,128]{3,2,1,0:T(8,128)S(1)} %get-tuple-element.24), channel_id=1, source_target_pairs={{1,2},{2,1},{5,6},{6,5},{9,10},{10,9},{13,14},{14,13},{17,18},{18,... | collective-permute-start | bytes 245768 | tf_op jit(solution)/shard_map/ppermute | solution.py:553
  28.5 4.4 %collective-permute-start.4 = (f32[32,128]{1,0:T(8,128)S(1)}, f32[32,128]{1,0:T(8,128)S(1)}, u32[]{:S(2)}, u32[]{:S(2)}) collective-permute-start(f32[32,128]{1,0:T(8,128)S(1)} %get-tuple-element.35.refs_0_), channel_id=1, source_target_pairs={{0,3},{1,2},{2,1},{3,0},{4,7},{5,6},{6,5},{7,4},{8,11},{9,10},{10,... | collective-permute-start | bytes 49160 | tf_op jit(solution)/shard_map/ppermute | solution.py:604
  29.5 5.2 %collective-permute-start.3 = (f32[32,128]{1,0:T(8,128)S(1)}, f32[32,128]{1,0:T(8,128)S(1)}, u32[]{:S(2)}, u32[]{:S(2)}) collective-permute-start(f32[32,128]{1,0:T(8,128)S(1)} %get-tuple-element.35.refs_0_), channel_id=1, source_target_pairs={{0,2},{1,3},{2,0},{3,1},{4,6},{5,7},{6,4},{7,5},{8,10},{9,11},{10,... | collective-permute-start | bytes 49160 | tf_op jit(solution)/shard_map/ppermute | solution.py:604
  32.9 1.9 %collective-permute-start.2 = (f32[32,128]{1,0:T(8,128)S(1)}, f32[32,128]{1,0:T(8,128)S(1)}, u32[]{:S(2)}, u32[]{:S(2)}) collective-permute-start(f32[32,128]{1,0:T(8,128)S(1)} %get-tuple-element.35.refs_0_), channel_id=1, source_target_pairs={{0,1},{1,0},{2,3},{3,2},{4,5},{5,4},{6,7},{7,6},{8,9},{9,8},{10,11... | collective-permute-start | bytes 49160 | tf_op jit(solution)/shard_map/ppermute | solution.py:604
